TPU v7x, 32 devices: a whole 2x2x4 slice. The times are simulated.
32 devices in a mesh: fsdp: 8 (over y, x, core), tp: 4 (over z).
Axes of the slice: x: 2, y: 2, z: 4, core: 2. Of those that a mesh axis runs over, the one named last changes fastest.
Arguments:
- hidden_in: bfloat16 [4096, 2048], P(('fsdp', 'tp')), may hold values from -6 to 6
- cotangent: bfloat16 [4096, 2048], P(('fsdp', 'tp')), may hold values from -6 to 6
- segment_ids: int32 [8, 512], P('fsdp'), may hold values from 0 to 3, never falling along the last dimension, each value on 1 to 256 neighbouring positions
- adapter_set: int32 [8], P('fsdp'), may hold values from 0 to 7
- qkv_weight: bfloat16 [3, 2048, 2048], P(None, 'fsdp', 'tp'), may hold values from -0.125 to 0.125
- qkv_bias: bfloat16 [2, 2048], P(None, 'tp'), may hold values from -3 to 3
- proj_weight: bfloat16 [2048, 2048], P('tp', 'fsdp'), may hold values from -1.5 to 1.5
- proj_bias: bfloat16 [2048], replicated, may hold values from -3 to 3
- up_weight: bfloat16 [2048, 8192], P('fsdp', 'tp'), may hold values from -0.125 to 0.125
- up_bias: bfloat16 [8192], P('tp'), may hold values from -3 to 3
- down_weight: bfloat16 [8192, 2048], P('tp', 'fsdp'), may hold values from -0.0625 to 0.0625
- down_bias: bfloat16 [2048], replicated, may hold values from -3 to 3
- norm_gain: bfloat16 [2, 2048], replicated, may hold values from 0.5 to 1.5
- norm_bias: bfloat16 [2, 2048], replicated, may hold values from -3 to 3
- qkv_adapt_in: bfloat16 [3, 8, 2048, 16], replicated, may hold values from -0.125 to 0.125
- qkv_adapt_out: bfloat16 [3, 8, 16, 2048], P(None, None, None, 'tp'), may hold values from -0.75 to 0.75
- attn_adapt_in: bfloat16 [8, 2048, 16], P(None, 'tp'), may hold values from -1.5 to 1.5
- attn_adapt_out: bfloat16 [8, 16, 2048], replicated, may hold values from -0.75 to 0.75
- up_adapt_in: bfloat16 [8, 2048, 16], replicated, may hold values from -0.125 to 0.125
- up_adapt_out: bfloat16 [8, 16, 8192], P(None, None, 'tp'), may hold values from -0.75 to 0.75
- down_adapt_in: bfloat16 [8, 8192, 16], P(None, 'tp'), may hold values from -0.0625 to 0.0625
- down_adapt_out: bfloat16 [8, 16, 2048], replicated, may hold values from -0.75 to 0.75
Outputs:
- layer_out: float32 [4096, 2048], P(('fsdp', 'tp'))
- grad_input: float32 [4096, 2048], P(('fsdp', 'tp'))
- grad_qkv_in: float32 [3, 8, 2048, 16], replicated
- grad_qkv_out: float32 [3, 8, 16, 2048], P(None, None, None, 'tp')
- grad_attn_in: float32 [8, 2048, 16], P(None, 'tp')
- grad_attn_out: float32 [8, 16, 2048], replicated
- grad_up_in: float32 [8, 2048, 16], replicated
- grad_up_out: float32 [8, 16, 8192], P(None, None, 'tp')
- grad_down_in: float32 [8, 8192, 16], P(None, 'tp')
- grad_down_out: float32 [8, 16, 2048], replicated
Inputs may be any that keep to these rules, and one draw needn't show every extreme that they name: `segment_ids`: within a sequence the numbers never fall; each of the 4 documents holds 1 to 256 tokens and one holds exactly 256.
All inputs are finite; a program needn't handle non-finite values.
Results may differ from a plain program's by a relative error of at most 0.018.
Values may be sent and summed in bfloat16 or wider, within the bound.
A program may use at most 192 MiB of HBM per device.

v0:
```python
import math

import jax
import jax.numpy as jnp
from jax import lax
from jax.sharding import PartitionSpec as P

HEAD = 128


def layer_norm(field_in, gain_row, shift_row):
    centre = jnp.mean(field_in, axis=-1, keepdims=True)
    centred = field_in - centre
    spread = jnp.mean(centred * centred, axis=-1, keepdims=True)
    return centred * lax.rsqrt(spread + 1e-05) * gain_row + shift_row


def precise_dot(left, right):
    return jnp.dot(left, right, precision=lax.Precision.HIGHEST)


def mixed_dot(left, right):
    return jnp.dot(left, right, preferred_element_type=jnp.float32)


def choose_set(table, index, axis):
    return lax.dynamic_index_in_dim(table, index, axis, keepdims=False)


def place_set(grad, index, sets, axis):
    onehot = (jnp.arange(sets) == index).astype(jnp.float32)
    shape_list = [1] * (grad.ndim + 1)
    shape_list[axis] = sets
    return jnp.expand_dims(grad, axis) * onehot.reshape(shape_list)


def per_device(
    hidden_in,
    cotangent,
    segment_ids,
    adapter_set,
    qkv_weight,
    qkv_bias,
    proj_weight,
    proj_bias,
    up_weight,
    up_bias,
    down_weight,
    down_bias,
    norm_gain,
    norm_bias,
    qkv_adapt_in,
    qkv_adapt_out,
    attn_adapt_in,
    attn_adapt_out,
    up_adapt_in,
    up_adapt_out,
    down_adapt_in,
    down_adapt_out,
):
    width_local = qkv_weight.shape[2]
    heads_local = width_local // HEAD
    sets = qkv_adapt_in.shape[1]
    chosen = adapter_set[0]
    segments = segment_ids[0]
    seq_rows = segments.shape[0]
    block_rows = min(512, seq_rows)
    blocks = seq_rows // block_rows
    score_scale = 1.0 / math.sqrt(HEAD)
    gains = norm_gain.astype(jnp.float32)
    shifts = norm_bias.astype(jnp.float32)
    first_q = choose_set(qkv_adapt_in, chosen, 1)
    second_q = choose_set(qkv_adapt_out, chosen, 1)
    first_o = choose_set(attn_adapt_in, chosen, 0)
    second_o = choose_set(attn_adapt_out, chosen, 0)
    first_u = choose_set(up_adapt_in, chosen, 0)
    second_u = choose_set(up_adapt_out, chosen, 0)
    first_d = choose_set(down_adapt_in, chosen, 0)
    second_d = choose_set(down_adapt_out, chosen, 0)
    seq_hidden = lax.all_gather(hidden_in, "tp", axis=0, tiled=True)
    qkv_full, proj_full = (
        lax.all_gather(qkv_weight, "fsdp", axis=1, tiled=True),
        lax.all_gather(proj_weight, "fsdp", axis=1, tiled=True),
    )
    main_term = jnp.einsum("sd,jdc->jsc", seq_hidden, qkv_full, preferred_element_type=jnp.float32)
    low_in = jnp.einsum("sd,jdr->jsr", seq_hidden, first_q, preferred_element_type=jnp.float32)
    low_term = jnp.einsum(
        "jsr,jrc->jsc", low_in, second_q.astype(jnp.float32), precision=lax.Precision.HIGHEST
    )
    bias_rows = jnp.stack([qkv_bias[0], jnp.zeros_like(qkv_bias[0]), qkv_bias[1]]).astype(
        jnp.float32
    )[:, None, :]
    qkv_round = (main_term + low_term + bias_rows).astype(jnp.bfloat16)
    queries = qkv_round[0].reshape(seq_rows, heads_local, HEAD)
    keys = qkv_round[1].reshape(seq_rows, heads_local, HEAD)
    values = qkv_round[2].reshape(seq_rows, heads_local, HEAD)
    query_blocks = queries.reshape(blocks, block_rows, heads_local, HEAD)
    seg_blocks = segments.reshape(blocks, block_rows)

    def scores_of(query_rows, seg_rows):
        raw_scores = (
            jnp.einsum("bhe,she->hbs", query_rows, keys, preferred_element_type=jnp.float32)
            * score_scale
        )
        same_doc = (seg_rows[:, None] == segments[None, :])[None]
        return jnp.where(same_doc, raw_scores, -1e30)

    def forward_block(inputs):
        query_rows, seg_rows = inputs
        scores = scores_of(query_rows, seg_rows)
        row_top = jnp.max(scores, axis=-1, keepdims=True)
        weights = jnp.exp(scores - row_top)
        row_total = jnp.sum(weights, axis=-1, keepdims=True)
        attn_probs = (weights / row_total).astype(jnp.bfloat16)
        attn_mixed = jnp.einsum(
            "hbs,she->bhe", attn_probs, values, preferred_element_type=jnp.float32
        )
        return (attn_mixed, (row_top + jnp.log(row_total))[..., 0])

    attn_mixed, logsum = lax.map(forward_block, (query_blocks, seg_blocks))
    attended = attn_mixed.reshape(seq_rows, width_local).astype(jnp.bfloat16)
    low_attn = mixed_dot(attended, first_o)
    second_o_wide = second_o.astype(jnp.float32)
    row_part = attended
    low_part = low_attn
    attn_sum = lax.psum_scatter(
        mixed_dot(row_part, proj_full) + precise_dot(low_part, second_o_wide),
        "tp",
        scatter_dimension=0,
        tiled=True,
    )
    first_sum = hidden_in.astype(jnp.float32) + attn_sum + proj_bias.astype(jnp.float32)
    normed = layer_norm(first_sum, gains[0], shifts[0])
    normed_round = normed.astype(jnp.bfloat16)
    seq_normed = lax.all_gather(normed_round, "tp", axis=0, tiled=True)
    up_full, down_full = (
        lax.all_gather(up_weight, "fsdp", axis=0, tiled=True),
        lax.all_gather(down_weight, "fsdp", axis=1, tiled=True),
    )
    low_up = mixed_dot(seq_normed, first_u)
    pre_act = (
        mixed_dot(seq_normed, up_full)
        + precise_dot(low_up, second_u.astype(jnp.float32))
        + up_bias.astype(jnp.float32)
    )
    act_round = jax.nn.gelu(pre_act, approximate=True).astype(jnp.bfloat16)
    low_down = mixed_dot(act_round, first_d)
    second_d_wide = second_d.astype(jnp.float32)
    row_part = act_round
    low_part = low_down
    ffn_sum = lax.psum_scatter(
        mixed_dot(row_part, down_full) + precise_dot(low_part, second_d_wide),
        "tp",
        scatter_dimension=0,
        tiled=True,
    )
    second_sum = normed + ffn_sum + down_bias.astype(jnp.float32)
    layer_out = layer_norm(second_sum, gains[1], shifts[1])
    unused, norm_back = jax.vjp(
        lambda field_in: layer_norm(field_in, gains[1], shifts[1]), second_sum
    )
    grad_second = norm_back(cotangent.astype(jnp.float32))[0]
    grad_feed_round = grad_second.astype(jnp.bfloat16)
    seq_grad_feed = lax.all_gather(grad_feed_round, "tp", axis=0, tiled=True)
    up_back, down_back = (
        lax.all_gather(up_weight, "fsdp", axis=0, tiled=True),
        lax.all_gather(down_weight, "fsdp", axis=1, tiled=True),
    )
    grad_low_down = mixed_dot(seq_grad_feed, second_d.T)
    grad_act = jnp.einsum(
        "sd,fd->sf", seq_grad_feed, down_back, preferred_element_type=jnp.float32
    ) + precise_dot(grad_low_down, first_d.astype(jnp.float32).T)
    unused, gelu_back = jax.vjp(lambda field_in: jax.nn.gelu(field_in, approximate=True), pre_act)
    grad_pre_round = gelu_back(grad_act)[0].astype(jnp.bfloat16)
    grad_down_out_part = precise_dot(low_down.T, seq_grad_feed.astype(jnp.float32))
    grad_down_in_part = precise_dot(act_round.astype(jnp.float32).T, grad_low_down)
    grad_low_up = mixed_dot(grad_pre_round, second_u.T)
    grad_up_out_part = precise_dot(low_up.T, grad_pre_round.astype(jnp.float32))
    grad_up_in_part = precise_dot(seq_normed.astype(jnp.float32).T, grad_low_up)
    first_u_wide = first_u.astype(jnp.float32)
    row_part = grad_pre_round
    low_part = grad_low_up
    grad_normed = grad_second + lax.psum_scatter(
        jnp.einsum("sf,df->sd", row_part, up_back, preferred_element_type=jnp.float32)
        + precise_dot(low_part, first_u_wide.T),
        "tp",
        scatter_dimension=0,
        tiled=True,
    )
    unused, norm_front = jax.vjp(
        lambda field_in: layer_norm(field_in, gains[0], shifts[0]), first_sum
    )
    grad_first = norm_front(grad_normed)[0]
    grad_branch_round = grad_first.astype(jnp.bfloat16)
    seq_grad_branch = lax.all_gather(grad_branch_round, "tp", axis=0, tiled=True)
    qkv_back, proj_back = (
        lax.all_gather(qkv_weight, "fsdp", axis=1, tiled=True),
        lax.all_gather(proj_weight, "fsdp", axis=1, tiled=True),
    )
    grad_low_attn = mixed_dot(seq_grad_branch, second_o.T)
    grad_attended = jnp.einsum(
        "sd,cd->sc", seq_grad_branch, proj_back, preferred_element_type=jnp.float32
    ) + precise_dot(grad_low_attn, first_o.astype(jnp.float32).T)
    grad_attended_round = grad_attended.astype(jnp.bfloat16)
    grad_attn_out_part = precise_dot(low_attn.T, seq_grad_branch.astype(jnp.float32))
    grad_attn_in_part = precise_dot(attended.astype(jnp.float32).T, grad_low_attn)
    grad_blocks = grad_attended_round.reshape(blocks, block_rows, heads_local, HEAD)

    def backward_block(carry, inputs):
        grad_keys, grad_values = carry
        query_rows, seg_rows, lse_rows, grad_rows = inputs
        scores = scores_of(query_rows, seg_rows)
        attn_probs = jnp.exp(scores - lse_rows[..., None])
        grad_probs = jnp.einsum(
            "bhe,she->hbs", grad_rows, values, preferred_element_type=jnp.float32
        )
        centre = jnp.sum(grad_probs * attn_probs, axis=-1, keepdims=True)
        grad_scores = (attn_probs * (grad_probs - centre)).astype(jnp.bfloat16)
        grad_query = (
            jnp.einsum("hbs,she->bhe", grad_scores, keys, preferred_element_type=jnp.float32)
            * score_scale
        )
        grad_keys = (
            grad_keys
            + jnp.einsum(
                "hbs,bhe->she", grad_scores, query_rows, preferred_element_type=jnp.float32
            )
            * score_scale
        )
        grad_values = grad_values + jnp.einsum(
            "hbs,bhe->she",
            attn_probs.astype(jnp.bfloat16),
            grad_rows,
            preferred_element_type=jnp.float32,
        )
        return ((grad_keys, grad_values), grad_query)

    zero_state = jnp.zeros((seq_rows, heads_local, HEAD), jnp.float32)
    key_value_grads, grad_queries = lax.scan(
        backward_block, (zero_state, zero_state), (query_blocks, seg_blocks, logsum, grad_blocks)
    )
    grad_qkv_round = jnp.stack(
        [
            grad_queries.reshape(seq_rows, width_local),
            key_value_grads[0].reshape(seq_rows, width_local),
            key_value_grads[1].reshape(seq_rows, width_local),
        ]
    ).astype(jnp.bfloat16)
    grad_qkv_out_part = jnp.einsum(
        "jsr,jsc->jrc", low_in, grad_qkv_round.astype(jnp.float32), precision=lax.Precision.HIGHEST
    )
    grad_low_qkv = jnp.einsum(
        "jsc,jrc->jsr", grad_qkv_round, second_q, preferred_element_type=jnp.float32
    )
    grad_qkv_in_part = jnp.einsum(
        "sd,jsr->jdr", seq_hidden.astype(jnp.float32), grad_low_qkv, precision=lax.Precision.HIGHEST
    )
    first_q_wide = first_q.astype(jnp.float32)
    row_part = grad_qkv_round
    low_part = grad_low_qkv
    grad_input = grad_first + lax.psum_scatter(
        (
            jnp.einsum("jsc,jdc->sd", row_part, qkv_back, preferred_element_type=jnp.float32)
            + jnp.einsum("jsr,jdr->sd", low_part, first_q_wide, precision=lax.Precision.HIGHEST)
        ).astype(jnp.bfloat16),
        "tp",
        scatter_dimension=0,
        tiled=True,
    ).astype(jnp.float32)
    wide_grads = lax.psum(
        (
            place_set(grad_qkv_in_part, chosen, sets, 1),
            place_set(grad_attn_out_part, chosen, sets, 0),
            place_set(grad_up_in_part, chosen, sets, 0),
            place_set(grad_down_out_part, chosen, sets, 0),
        ),
        ("fsdp", "tp"),
    )
    split_grads = (
        lax.psum(place_set(grad_qkv_out_part, chosen, sets, 1).astype(jnp.bfloat16), "fsdp").astype(
            jnp.float32
        ),
        lax.psum(place_set(grad_attn_in_part, chosen, sets, 0).astype(jnp.bfloat16), "fsdp").astype(
            jnp.float32
        ),
        lax.psum(place_set(grad_up_out_part, chosen, sets, 0).astype(jnp.bfloat16), "fsdp").astype(
            jnp.float32
        ),
        lax.psum(place_set(grad_down_in_part, chosen, sets, 0).astype(jnp.bfloat16), "fsdp").astype(
            jnp.float32
        ),
    )
    return (
        layer_out,
        grad_input,
        wide_grads[0],
        split_grads[0],
        split_grads[1],
        wide_grads[1],
        wide_grads[2],
        split_grads[2],
        split_grads[3],
        wide_grads[3],
    )


def solution(mesh):
    placed = (
        P(("fsdp", "tp"), None),
        P(("fsdp", "tp"), None),
        P("fsdp", None),
        P("fsdp"),
        P(None, "fsdp", "tp"),
        P(None, "tp"),
        P("tp", "fsdp"),
        P(),
        P("fsdp", "tp"),
        P("tp"),
        P("tp", "fsdp"),
        P(),
        P(),
        P(),
        P(),
        P(None, None, None, "tp"),
        P(None, "tp", None),
        P(),
        P(),
        P(None, None, "tp"),
        P(None, "tp", None),
        P(),
    )
    return jax.shard_map(
        per_device,
        mesh=mesh,
        in_specs=placed,
        out_specs=(
            P(("fsdp", "tp"), None),
            P(("fsdp", "tp"), None),
            P(),
            P(None, None, None, "tp"),
            P(None, "tp", None),
            P(),
            P(),
            P(None, None, "tp"),
            P(None, "tp", None),
            P(),
        ),
        check_vma=False,
    )
```

profile of v0, /device:TPU:0, one launch (start us, length us, event | category | flops | bytes accessed | tf_op | source)
XLA Modules:
  0.0 984.8 jit_solution(15811532477043070335)
XLA Ops:
  13.6 44.6 %all-gather.11.cloned.1.call-done = bf16[512,2048]{1,0:T(8,128)(2,1)} async-done(((bf16[128,2048]{1,0:T(8,128)(2,1)}), bf16[512,2048]{1,0:T(8,128)(2,1)}) %all-gather.11.cloned.1.call-update) | async-done | bytes 2097168 | tf_op jit(solution)/shard_map/all_gather | solution.py:80
  60.6 45.5 %all-gather.9.cloned.1.call-done = bf16[3,2048,512]{1,2,0:T(8,128)(2,1)} async-done(((bf16[3,256,512]{1,2,0:T(8,128)(2,1)}), bf16[3,2048,512]{1,2,0:T(8,128)(2,1)}) %all-gather.9.cloned.1.call-update) | async-done | bytes 6291472 | tf_op jit(solution)/shard_map/all_gather | solution.py:82
  106.1 6.2 fusion.17
  118.8 17.4 %all-gather.13.cloned.1.call-done = bf16[512,2048]{1,0:T(8,128)(2,1)} async-done(((bf16[512,256]{1,0:T(8,128)(2,1)}), bf16[512,2048]{1,0:T(8,128)(2,1)}) %all-gather.13.cloned.1.call-update) | async-done | bytes 2097168 | tf_op jit(solution)/shard_map/all_gather | solution.py:83
  136.2 2.9 fusion.97
  139.1 4.8 convolution_add_fusion.2
  144.7 76.2 %reduce-scatter.5.cloned.1.call-done = f32[128,2048]{1,0:T(8,128)} async-done(((f32[512,2048]{1,0:T(8,128)}), f32[128,2048]{1,0:T(8,128)}) %reduce-scatter.5.cloned.1.call-update) | async-done | bytes 1048592 | tf_op jit(solution)/shard_map/reduce_scatter | solution.py:126
  225.7 44.8 %all-gather.15.cloned.1.call-done = bf16[512,2048]{1,0:T(8,128)(2,1)} async-done(((bf16[128,2048]{1,0:T(8,128)(2,1)}), bf16[512,2048]{1,0:T(8,128)(2,1)}) %all-gather.15.cloned.1.call-update) | async-done | bytes 2097168 | tf_op jit(solution)/shard_map/all_gather | solution.py:135
  272.6 52.8 %all-gather.17.cloned.1.call-done = bf16[2048,2048]{1,0:T(8,128)(2,1)} async-done(((bf16[256,2048]{1,0:T(8,128)(2,1)}), bf16[2048,2048]{1,0:T(8,128)(2,1)}) %all-gather.17.cloned.1.call-update) | async-done | bytes 8388624 | tf_op jit(solution)/shard_map/all_gather | solution.py:137
  325.5 7.6 fusion.98
  333.0 6.1 multiply_convert_fusion.1
  342.0 41.5 %all-gather.19.cloned.1.call-done = bf16[2048,2048]{1,0:T(8,128)(2,1)} async-done(((bf16[2048,256]{1,0:T(8,128)(2,1)}), bf16[2048,2048]{1,0:T(8,128)(2,1)}) %all-gather.19.cloned.1.call-update) | async-done | bytes 8388624 | tf_op jit(solution)/shard_map/all_gather | solution.py:138
  383.5 7.6 fusion.99
  391.0 4.7 convolution_add_fusion.1
  396.4 76.2 %reduce-scatter.7.cloned.1.call-done = f32[128,2048]{1,0:T(8,128)} async-done(((f32[512,2048]{1,0:T(8,128)}), f32[128,2048]{1,0:T(8,128)}) %reduce-scatter.7.cloned.1.call-update) | async-done | bytes 1048592 | tf_op jit(solution)/shard_map/reduce_scatter | solution.py:151
  479.4 46.4 %all-gather.21.cloned.1.call-done = bf16[512,2048]{1,0:T(8,128)(2,1)} async-done(((bf16[128,2048]{1,0:T(8,128)(2,1)}), bf16[512,2048]{1,0:T(8,128)(2,1)}) %all-gather.21.cloned.1.call-update) | async-done | bytes 2097168 | tf_op jit(solution)/shard_map/all_gather | solution.py:164
  525.7 8.6 fusion.100
  536.0 5.8 fusion.6
  543.4 4.5 fusion.101
  548.0 4.8 convolution_add_fusion
  552.8 75.6 %reduce-scatter.9.cloned.1.call-done = f32[128,2048]{1,0:T(8,128)} async-done(((f32[512,2048]{1,0:T(8,128)}), f32[128,2048]{1,0:T(8,128)}) %reduce-scatter.9.cloned.1.call-update) | async-done | bytes 1048592 | tf_op jit(solution)/shard_map/reduce_scatter | solution.py:183
  634.6 2.7 fusion.107
  637.2 2.5 fusion.106
  643.0 38.1 %all-gather.23.cloned.1.call-done = bf16[512,2048]{1,0:T(8,128)(2,1)} async-done(((bf16[128,2048]{1,0:T(8,128)(2,1)}), bf16[512,2048]{1,0:T(8,128)(2,1)}) %all-gather.23.cloned.1.call-update) | async-done | bytes 2097168 | tf_op jit(solution)/shard_map/all_gather | solution.py:195
  683.8 3.7 fusion.102
  704.2 5.7 fusion.87
  711.2 3.5 fusion.7
  714.8 2.8 convolution_bitcast_fusion
  719.7 42.1 %all-reduce.7.cloned.1.call-done = (bf16[3,8,16,512]{3,2,1,0:T(8,128)(2,1)}, bf16[8,512,16]{1,2,0:T(8,128)(2,1)}, bf16[8,16,2048]{2,1,0:T(8,128)(2,1)}, bf16[8,2048,16]{1,2,0:T(8,128)(2,1)}) async-done(((bf16[3,8,16,512]{3,2,1,0:T(8,128)(2,1)}, bf16[8,512,16]{1,2,0:T(8,128)(2,1)}, bf16[8,16,2048]{2,1,0:T(8,128)(2,1)}, bf16[8,2048,16]{1,2,0:T(8,128)(2,1)}), (bf16[3,8,16,512]{3,2,1,0:T(8,128)(2,1)}, ...) | async-done | bytes 1572880 | tf_op jit(solution)/shard_map/psum | solution.py:280
  769.7 37.7 %reduce-scatter.11.cloned.1.call-done = bf16[128,2048]{1,0:T(8,128)(2,1)} async-done(((bf16[512,2048]{1,0:T(8,128)(2,1)}), bf16[128,2048]{1,0:T(8,128)(2,1)}) %reduce-scatter.11.cloned.1.call-update) | async-done | bytes 524304 | tf_op jit(solution)/shard_map/reduce_scatter | solution.py:261
  809.6 161.3 %all-reduce.5.cloned.1.call-done = (f32[3,8,2048,16]{2,3,1,0:T(8,128)}, f32[8,16,2048]{2,1,0:T(8,128)}, f32[8,2048,16]{1,2,0:T(8,128)}, f32[8,16,2048]{2,1,0:T(8,128)}) async-done(((f32[3,8,2048,16]{2,3,1,0:T(8,128)}, f32[8,16,2048]{2,1,0:T(8,128)}, f32[8,2048,16]{1,2,0:T(8,128)}, f32[8,16,2048]{2,1,0:T(8,128)}), (f32[3,8,2048,16]{2,3,1,0:T(8,128)}, f32[8,16,2048]{2,1,0:T(8,128)}, f32[8,2048,16]{1,2,0:T(8,128)}, ...) | async-done | bytes 6291472 | tf_op jit(solution)/shard_map/psum | solution.py:270
  970.9 4.1 copy.63
  (178 shorter events, 80.6 us)
Async XLA Ops:
  7.2 51.1 %copy-start = (bf16[3,8,2048,16]{2,3,1,0:T(8,128)(2,1)S(1)}, bf16[3,8,2048,16]{2,3,1,0:T(8,128)(2,1)}, u32[]{:S(2)}) copy-start(bf16[3,8,2048,16]{2,3,1,0:T(8,128)(2,1)} %param.36) | copy-start | bytes 4718596
  7.2 51.1 %all-gather.11.cloned.1.call-start = ((), (), s32[]{:S(2)}) async-start(), calls=%async_computation.5 | async-start | bytes 2621440 | tf_op jit(solution)/shard_map/all_gather | solution.py:80
  7.9 98.2 %all-gather.9.cloned.1.call-start = ((), (), s32[]{:S(2)}) async-start(), calls=%async_computation.4 | async-start | bytes 7077888 | tf_op jit(solution)/shard_map/all_gather | solution.py:82
  10.3 126.0 %all-gather.13.cloned.1.call-start = ((), (), s32[]{:S(2)}) async-start(), calls=%async_computation.6 | async-start | bytes 2359296 | tf_op jit(solution)/shard_map/all_gather | solution.py:83
  11.0 209.8 %reduce-scatter.5.cloned.1.call-start = ((), (), s32[]{:S(2)}) async-start(), calls=%async_computation.7 | async-start | bytes 5242880 | tf_op jit(solution)/shard_map/reduce_scatter | solution.py:126
  118.8 25.1 %copy-start.30 = (f32[512,16]{0,1:T(8,128)}, f32[512,16]{0,1:T(8,128)S(1)}, u32[]{:S(2)}) copy-start(f32[512,16]{0,1:T(8,128)S(1)} %fusion.64) | copy-start | bytes 98308
  143.9 81.7 %copy-start.35 = (bf16[2048]{0:T(1024)(128)(2,1)S(1)}, bf16[2048]{0:T(1024)(128)(2,1)}, u32[]{:S(2)}) copy-start(bf16[2048]{0:T(1024)(128)(2,1)} %param.31) | copy-start | bytes 12292
  144.0 126.5 %all-gather.15.cloned.1.call-start = ((), (), s32[]{:S(2)}) async-start(), calls=%async_computation.8 | async-start | bytes 2621440 | tf_op jit(solution)/shard_map/all_gather | solution.py:135
  223.8 101.7 %all-gather.17.cloned.1.call-start = ((), (), s32[]{:S(2)}) async-start(), calls=%async_computation.9 | async-start | bytes 9437184 | tf_op jit(solution)/shard_map/all_gather | solution.py:137
  224.4 159.1 %all-gather.19.cloned.1.call-start = ((), (), s32[]{:S(2)}) async-start(), calls=%async_computation.10 | async-start | bytes 9437184 | tf_op jit(solution)/shard_map/all_gather | solution.py:138
  225.1 247.5 %reduce-scatter.7.cloned.1.call-start = ((), (), s32[]{:S(2)}) async-start(), calls=%async_computation.11 | async-start | bytes 5242880 | tf_op jit(solution)/shard_map/reduce_scatter | solution.py:151
  395.8 130.0 %all-gather.21.cloned.1.call-start = ((), (), s32[]{:S(2)}) async-start(), calls=%async_computation.12 | async-start | bytes 2621440 | tf_op jit(solution)/shard_map/all_gather | solution.py:164
  479.1 149.3 %reduce-scatter.9.cloned.1.call-start = ((), (), s32[]{:S(2)}) async-start(), calls=%async_computation.13 | async-start | bytes 5242880 | tf_op jit(solution)/shard_map/reduce_scatter | solution.py:183
  525.7 8.6 copy-start.8
  525.7 10.2 %copy-start.37 = (f32[512,2048]{1,0:T(8,128)S(1)}, f32[512,2048]{1,0:T(8,128)}, u32[]{:S(2)}) copy-start(f32[512,2048]{1,0:T(8,128)} %get-tuple-element.99) | copy-start | bytes 12582916
  534.3 9.1 slice-start
  536.0 7.4 slice-start.1
  541.8 6.1 copy-start.11
  543.4 4.6 copy-start.28
  552.8 128.3 %all-gather.23.cloned.1.call-start = ((), (), s32[]{:S(2)}) async-start(), calls=%async_computation.14 | async-start | bytes 2621440 | tf_op jit(solution)/shard_map/all_gather | solution.py:195
  633.3 7.4 copy-start.29
  634.3 127.6 %all-reduce.7.cloned.1.call-start = ((), (), s32[]{:S(2)}) async-start(), calls=%async_computation.17 | async-start | bytes 3145728 | tf_op jit(solution)/shard_map/psum | solution.py:280
  634.5 5.2 copy-start.9
  634.5 6.2 copy-start.6
  683.8 5.1 copy-start.2
  694.9 6.3 copy-start.31
  703.9 103.5 %reduce-scatter.11.cloned.1.call-start = ((), (), s32[]{:S(2)}) async-start(), calls=%async_computation.15 | async-start | bytes 2621440 | tf_op jit(solution)/shard_map/reduce_scatter | solution.py:261
  704.2 5.7 copy-start.27
  714.7 256.1 %all-reduce.5.cloned.1.call-start = ((), (), s32[]{:S(2)}) async-start(), calls=%async_computation.16 | async-start | bytes 12582912 | tf_op jit(solution)/shard_map/psum | solution.py:270
  719.7 87.7 %copy-start.5 = (f32[128,2048]{1,0:T(8,128)S(1)}, f32[128,2048]{1,0:T(8,128)}, u32[]{:S(2)}) copy-start(f32[128,2048]{1,0:T(8,128)} %copy-done.4) | copy-start | bytes 3145732
  970.9 5.0 copy-start.21
  970.9 6.0 copy-start.20
  (22 other events, 46.4 us)
Sparse Core Ops, SparseCore 0:
  9.6 48.6 all-gather.10
  60.7 45.3 all-gather.8
  108.0 28.1 all-gather.12
  144.1 76.7 reduce-scatter.4
  223.9 46.4 all-gather.14
  272.3 53.0 all-gather.16
  327.5 55.9 all-gather.18
  395.9 76.7 reduce-scatter.6
  479.3 46.4 all-gather.20
  552.9 75.4 reduce-scatter.8
  634.4 46.6 all-gather.22
  704.0 57.7 all-reduce.6
  764.1 43.2 reduce-scatter.10
  814.9 155.9 all-reduce.4
where the time goes:
time: 993 us; the launch traced here: 985 us
  waiting for transfers between devices  803 us (81%)
  matrix products  114 us (11%)
  other arithmetic  32.9 us (3%)
  local copies, waits for them, and re-layouts  18 us (2%)
  between operations  15.6 us (2%)
    psum x1, waiting for transfers between devices, per_device(): lax.psum((place_set(grad_qkv_in_part, chosen, sets, 1), place_set(grad_at...  161 us
    reduce_scatter x1, waiting for transfers between devices, per_device(): lax.psum_scatter(mixed_dot(row_part, down_full) + precise_dot(low_part, s...  76.2 us
    reduce_scatter x1, waiting for transfers between devices, per_device(): lax.psum_scatter(mixed_dot(row_part, proj_full) + precise_dot(low_part, s...  76.2 us
    reduce_scatter x1, waiting for transfers between devices, per_device(): lax.psum_scatter(jnp.einsum('sf,df->sd', row_part, up_back, preferred_ele...  75.6 us
    all_gather x1, waiting for transfers between devices, per_device(): lax.all_gather(up_weight, 'fsdp', axis=0, tiled=True)  52.8 us
    all_gather x1, waiting for transfers between devices, per_device(): seq_grad_feed = lax.all_gather(grad_feed_round, 'tp', axis=0, tiled=True)  46.4 us
    all_gather x1, waiting for transfers between devices, per_device(): lax.all_gather(qkv_weight, 'fsdp', axis=1, tiled=True)  45.5 us
    all_gather x1, waiting for transfers between devices, per_device(): seq_normed = lax.all_gather(normed_round, 'tp', axis=0, tiled=True)  44.8 us
  transfers between devices with their start and end apart: 14, of which 14 were waited for; matrix products, arithmetic and copies ran while one was open for 7% of the time, Pallas kernels for 0%

commit v1 on v0

--- a/solution.py
+++ b/solution.py
@@ -1,11 +1,19 @@
+import functools
 import math
 
 import jax
 import jax.numpy as jnp
 from jax import lax
+from jax.experimental import pallas as pl
+from jax.experimental.pallas import tpu as pltpu
 from jax.sharding import PartitionSpec as P
 
 HEAD = 128
+RANK = 16
+MESH = pl.DeviceIdType.MESH
+F32 = jnp.float32
+BF16 = jnp.bfloat16
+ROOT = math.sqrt(2.0 / math.pi)
 
 
 def layer_norm(field_in, gain_row, shift_row):
@@ -304,7 +312,588 @@
     )
 
 
-def solution(mesh):
+def dot_nn(left, right):
+    return jnp.dot(left, right, preferred_element_type=F32)
+
+
+def dot_nt(left, right):
+    return lax.dot_general(left, right, (((1,), (1,)), ((), ())), preferred_element_type=F32)
+
+
+def flip(index, mask):
+    out, bit = index, 1
+    while bit <= mask:
+        if mask & bit:
+            out = out + bit - 2 * bit * lax.rem(lax.div(index, bit), 2)
+        bit *= 2
+    return out
+
+
+def norm_parts(rows):
+    centred = rows - jnp.mean(rows, axis=-1, keepdims=True)
+    spread = jnp.mean(centred * centred, axis=-1, keepdims=True)
+    rstd = lax.rsqrt(spread + 1e-05)
+    return centred * rstd, rstd
+
+
+def norm_pull(grad, unit, rstd):
+    return rstd * (
+        grad
+        - jnp.mean(grad, axis=-1, keepdims=True)
+        - unit * jnp.mean(grad * unit, axis=-1, keepdims=True)
+    )
+
+
+class Gather:
+    def __init__(self, which, shard, whole, send, recv, fsdp, tp, count):
+        self.which, self.shard, self.whole = which, shard, whole
+        self.send, self.recv, self.fsdp, self.tp = send, recv, fsdp, tp
+        bits = [1 << i for i in range(1, count.bit_length() - 1)]
+        self.orders = [bits, bits[::-1]]
+        self.steps = len(bits)
+        self.held = [[0], [0]]
+        self.sent = []
+        self.count = count
+
+    def copy(self, half, mask, bit):
+        landed = mask ^ bit
+        place = self.whole(flip(self.fsdp, mask), half)
+        return pltpu.make_async_remote_copy(
+            src_ref=self.shard(half) if mask == 0 else place,
+            dst_ref=place,
+            send_sem=self.send.at[self.which, half, landed],
+            recv_sem=self.recv.at[self.which, half, landed],
+            device_id=(flip(self.fsdp, bit), self.tp),
+            device_id_type=MESH,
+        )
+
+    def launch(self, half, mask, bit):
+        self.copy(half, mask, bit).start()
+        self.sent.append((half, mask, bit))
+
+    def await_block(self, half, mask, bit):
+        place = self.whole(flip(self.fsdp, mask), half)
+        pltpu.make_async_remote_copy(
+            src_ref=place,
+            dst_ref=place,
+            send_sem=self.send.at[self.which, half, mask],
+            recv_sem=self.recv.at[self.which, half, mask],
+            device_id=(flip(self.fsdp, bit), self.tp),
+            device_id_type=MESH,
+        ).wait_recv()
+
+    def stage(self, step):
+        for half in range(2):
+            fresh = [0]
+            if step > 0:
+                bit = self.orders[half][step - 1]
+                fresh = [mask ^ bit for mask in self.held[half]]
+                for mask in fresh:
+                    self.await_block(half, mask, bit)
+                self.held[half] = self.held[half] + fresh
+            if step < self.steps:
+                for mask in self.held[half]:
+                    self.launch(half, mask, self.orders[half][step])
+            for mask in fresh:
+                self.launch(half, mask, 1)
+
+    def finish(self):
+        for half in range(2):
+            for mask in self.held[half]:
+                self.await_block(half, mask ^ 1, 1)
+
+    def drain(self):
+        for half, mask, bit in self.sent:
+            self.copy(half, mask, bit).wait_send()
+
+
+def layer_kernel(cfg, *refs):
+    F, T, S, D, H, FL, C = (cfg[k] for k in ("F", "T", "S", "D", "H", "FL", "C"))
+    Q, heads, block = S // T, H // HEAD, D // F
+    R = Q // C
+    M = T * R
+    NT = min(256, FL)
+    (
+        hidden_in, cotangent, seg_row, seg_col, qkv_w, proj_w, up_w, down_w,
+        vectors, up_bias, qkv_bias, wide_f, heads_f, units_f,
+        layer_out, grad_input, wide_g, heads_g, units_g,
+        hidden, qkv_all, proj_all, up_all, down_all,
+        qkv, probs, mixed, normed, act, slope, grad_feed, grad_pre, grad_branch, grad_mixed, grad_qkv,
+        part, from_low, from_high, unit_one, rstd_one, grad_own,
+        low_q, low_o, low_u, low_d, back_q, back_o, back_u, back_d,
+        w_send, w_recv, up_send, up_recv, dn_send, dn_recv, g_up_send, g_up_recv, g_dn_send, g_dn_recv,
+        own_sem,
+    ) = refs
+    f, z = lax.axis_index("fsdp"), lax.axis_index("tp")
+    bits = [1 << i for i in range(F.bit_length() - 1)]
+
+    barrier = pltpu.get_barrier_semaphore()
+    for bit in bits:
+        pl.semaphore_signal(barrier, inc=1, device_id=(flip(f, bit), z), device_id_type=MESH)
+
+    @pl.when(z > 0)
+    def _():
+        pl.semaphore_signal(barrier, inc=1, device_id=(f, z - 1), device_id_type=MESH)
+
+    @pl.when(z < T - 1)
+    def _():
+        pl.semaphore_signal(barrier, inc=1, device_id=(f, z + 1), device_id_type=MESH)
+
+    inside = (z > 0) & (z < T - 1)
+
+    @pl.when(inside)
+    def _():
+        pl.semaphore_wait(barrier, len(bits) + 2)
+
+    @pl.when(jnp.logical_not(inside))
+    def _():
+        pl.semaphore_wait(barrier, len(bits) + 1)
+
+    rows_of = lambda total, half: pl.ds(half * (total // 2), total // 2)
+    gathers = [
+        Gather(0, lambda h: qkv_w.at[:, rows_of(block, h)], lambda g, h: qkv_all.at[:, g, rows_of(block, h)], w_send, w_recv, f, z, F),
+        Gather(1, lambda h: proj_w.at[rows_of(H, h)], lambda g, h: proj_all.at[g, rows_of(H, h)], w_send, w_recv, f, z, F),
+        Gather(2, lambda h: up_w.at[rows_of(block, h)], lambda g, h: up_all.at[g, rows_of(block, h)], w_send, w_recv, f, z, F),
+        Gather(3, lambda h: down_w.at[rows_of(FL, h)], lambda g, h: down_all.at[g, rows_of(FL, h)], w_send, w_recv, f, z, F),
+    ]
+    K = gathers[0].steps
+    own_copies = [
+        pltpu.make_async_copy(hidden_in, hidden.at[:, z], own_sem.at[0]),
+        pltpu.make_async_copy(qkv_w, qkv_all.at[:, f], own_sem.at[1]),
+        pltpu.make_async_copy(proj_w, proj_all.at[f], own_sem.at[2]),
+        pltpu.make_async_copy(up_w, up_all.at[f], own_sem.at[3]),
+        pltpu.make_async_copy(down_w, down_all.at[f], own_sem.at[4]),
+    ]
+
+    def line_copy(src, dst, send, recv, c, q, step):
+        return pltpu.make_async_remote_copy(
+            src_ref=src, dst_ref=dst, send_sem=send.at[c, q], recv_sem=recv.at[c, q],
+            device_id=(f, z + step), device_id_type=MESH,
+        )
+
+    def rs_copy(c, q, step):
+        landing, send, recv = (from_low, up_send, up_recv) if step > 0 else (from_high, dn_send, dn_recv)
+        return line_copy(part.at[c, q], landing.at[c, q], send, recv, c, q, step)
+
+    def rs_wait(c, q, step):
+        landing, send, recv = (from_low, up_send, up_recv) if step > 0 else (from_high, dn_send, dn_recv)
+        line_copy(landing.at[c, q], landing.at[c, q], send, recv, c, q, -step).wait_recv()
+
+    def rs(c, t):
+        def add(q, landing):
+            part[c, q] = (part[c, q].astype(F32) + landing[c, q].astype(F32)).astype(BF16)
+
+        @pl.when(z <= t - 1)
+        def _():
+            q = T - t + z
+
+            @pl.when(z > 0)
+            def _():
+                rs_wait(c, q, 1)
+                add(q, from_low)
+
+            rs_copy(c, q, 1).start()
+
+        @pl.when(z >= T - t)
+        def _():
+            q = z - (T - t)
+
+            @pl.when(z < T - 1)
+            def _():
+                rs_wait(c, q, -1)
+                add(q, from_high)
+
+            rs_copy(c, q, -1).start()
+
+    def rs_sum(c):
+        @pl.when(z > 0)
+        def _():
+            rs_wait(c, z, 1)
+
+        @pl.when(z < T - 1)
+        def _():
+            rs_wait(c, z, -1)
+
+        return (part[c, z].astype(F32) + from_low[c, z].astype(F32)) + from_high[c, z].astype(F32)
+
+    def rs_drain(c):
+        for q in range(T):
+            if q > 0:
+
+                @pl.when(z < q)
+                def _(q=q):
+                    rs_copy(c, q, 1).wait_send()
+
+            if q < T - 1:
+
+                @pl.when(z > q)
+                def _(q=q):
+                    rs_copy(c, q, -1).wait_send()
+
+    def ag_copy(buffer, c, q, step):
+        send, recv = (g_up_send, g_up_recv) if step > 0 else (g_dn_send, g_dn_recv)
+        if c is None:
+            return line_copy(buffer.at[:, q], buffer.at[:, q], send, recv, C, q, step)
+        return line_copy(buffer.at[c, q], buffer.at[c, q], send, recv, c, q, step)
+
+    def ag_wait(buffer, c, q, step):
+        send, recv = (g_up_send, g_up_recv) if step > 0 else (g_dn_send, g_dn_recv)
+        place = buffer.at[:, q] if c is None else buffer.at[c, q]
+        line_copy(place, place, send, recv, C if c is None else c, q, -step).wait_recv()
+
+    def ag(buffer, c, t):
+        if t == 1:
+
+            @pl.when(z < T - 1)
+            def _():
+                ag_copy(buffer, c, z, 1).start()
+
+            @pl.when(z > 0)
+            def _():
+                ag_copy(buffer, c, z, -1).start()
+
+            return
+
+        @pl.when(z >= t - 1)
+        def _():
+            q = z - (t - 1)
+            ag_wait(buffer, c, q, 1)
+
+            @pl.when(z < T - 1)
+            def _():
+                ag_copy(buffer, c, q, 1).start()
+
+        @pl.when(z <= T - t)
+        def _():
+            q = z + (t - 1)
+            ag_wait(buffer, c, q, -1)
+
+            @pl.when(z > 0)
+            def _():
+                ag_copy(buffer, c, q, -1).start()
+
+    def ag_drain(buffer, c):
+        for q in range(T):
+
+            @pl.when((z >= q) & (z < T - 1))
+            def _(q=q):
+                ag_copy(buffer, c, q, 1).wait_send()
+
+            @pl.when((z <= q) & (z > 0))
+            def _(q=q):
+                ag_copy(buffer, c, q, -1).wait_send()
+
+    a_q = lambda j: wide_f.at[pl.ds(16 * j, 16)]
+    b_o, a_u, b_d = (wide_f.at[pl.ds(16 * k, 16)] for k in (3, 4, 5))
+    b_q = lambda j: heads_f.at[pl.ds(16 * j, 16)]
+    a_o = heads_f.at[pl.ds(48, 16)]
+    b_u, a_d = (units_f.at[pl.ds(16 * k, 16)] for k in (0, 1))
+    v_proj, v_down, gain_a, shift_a, gain_b, shift_b = (vectors.at[pl.ds(k, 1)] for k in range(6))
+
+    def chunk(buffer, c):
+        return buffer[c].reshape(M, buffer.shape[-1])
+
+    def cols_of(g, size):
+        return pl.ds(pl.multiple_of(g * size, size), size)
+
+    def project():
+        width = min(256, H)
+        for j in range(3):
+            low_j = dot_nt(hidden[...].reshape(S, D), a_q(j)[...]).astype(BF16)
+            low_q[j] = low_j
+
+            @pl.loop(0, H // width)
+            def _(n, j=j, low_j=low_j):
+                cols = cols_of(n, width)
+                rows = dot_nn(hidden[...].reshape(S, D), qkv_all[j, :, :, cols].reshape(D, width))
+                rows += dot_nn(low_j, b_q(j)[:, cols]) + qkv_bias[pl.ds(j, 1), cols]
+                qkv[j, :, cols] = rows.astype(BF16)
+
+    scale = 1.0 / math.sqrt(HEAD)
+
+    def attend():
+        @pl.loop(0, heads)
+        def _(h):
+            cols = cols_of(h, HEAD)
+            value_t = qkv[2, :, cols].T
+            width = min(256, S)
+
+            @pl.loop(0, S // width)
+            def _(n):
+                rows = cols_of(n, width)
+                scores = dot_nt(qkv[1, :, cols], qkv[0, rows, cols]) * scale
+                scores = jnp.where(seg_col[...] == seg_row[:, rows], scores, -1e30)
+                weights = jnp.exp(scores - jnp.max(scores, axis=0, keepdims=True))
+                weights = weights * (1.0 / jnp.sum(weights, axis=0, keepdims=True))
+                low = weights.astype(BF16)
+                probs[h, :, rows] = low
+                mixed[rows, cols] = dot_nn(value_t, low).T.astype(BF16)
+
+    def attend_back():
+        @pl.loop(0, heads)
+        def _(h):
+            cols = cols_of(h, HEAD)
+            key_t = qkv[1, :, cols].T
+            width = min(256, S)
+
+            @pl.loop(0, S // width)
+            def _(n):
+                rows = cols_of(n, width)
+                weights = probs[h, :, rows].astype(F32)
+                grad = dot_nt(qkv[2, :, cols], grad_mixed[rows, cols])
+                centre = jnp.sum(grad * weights, axis=0, keepdims=True)
+                low = (weights * (grad - centre)).astype(BF16)
+                grad_scores[:, rows] = low
+                grad_qkv[0, rows, cols] = (dot_nn(key_t, low).T * scale).astype(BF16)
+
+            grad_qkv[1, :, cols] = (dot_nn(grad_scores[...], qkv[0, :, cols]) * scale).astype(BF16)
+            grad_qkv[2, :, cols] = dot_nn(probs[h], grad_mixed[:, cols]).astype(BF16)
+
+    grad_scores = slope.at[pl.ds(0, S), pl.ds(0, S)]
+
+    def span(c):
+        return pl.ds(c * M, M)
+
+    def put_part(c, cols, rows):
+        part[c, :, :, cols] = rows.astype(BF16).reshape(T, R, rows.shape[-1])
+
+    def mix_out(c):
+        low = dot_nt(mixed[span(c)], a_o[...]).astype(BF16)
+        low_o[span(c)] = low
+
+        @pl.loop(0, F)
+        def _(g):
+            cols = cols_of(g, block)
+            put_part(c, cols, dot_nn(mixed[span(c)], proj_all[g]) + dot_nn(low, b_o[:, cols]))
+
+    def feed_up(c):
+        low = dot_nt(chunk(normed, c), a_u[...]).astype(BF16)
+        low_u[span(c)] = low
+
+        @pl.loop(0, FL // NT)
+        def _(n):
+            cols = cols_of(n, NT)
+            pre = dot_nn(chunk(normed, c), up_all[:, :, cols].reshape(D, NT))
+            pre += dot_nn(low, b_u[:, cols]) + up_bias[:, cols]
+            square = pre * pre
+            bend = jnp.tanh(ROOT * (pre + 0.044715 * square * pre))
+            half = 0.5 * (1.0 + bend)
+            act[span(c), cols] = (pre * half).astype(BF16)
+            rise = half + 0.5 * pre * (1.0 - bend * bend) * (ROOT * (1.0 + 3 * 0.044715 * square))
+            slope[span(c), cols] = rise.astype(BF16)
+
+    def feed_down(c):
+        low = dot_nt(act[span(c)], a_d[...]).astype(BF16)
+        low_d[span(c)] = low
+
+        @pl.loop(0, F)
+        def _(g):
+            cols = cols_of(g, block)
+            put_part(c, cols, dot_nn(act[span(c)], down_all[g]) + dot_nn(low, b_d[:, cols]))
+
+    def back_down(c):
+        low = dot_nt(chunk(grad_feed, c), b_d[...]).astype(BF16)
+        back_d[span(c)] = low
+
+        @pl.loop(0, FL // NT)
+        def _(n):
+            cols = cols_of(n, NT)
+            total = dot_nn(low, a_d[:, cols])
+            for g in range(F):
+                rows = grad_feed[c, :, :, pl.ds(g * block, block)].reshape(M, block)
+                total += dot_nt(rows, down_all[g, cols])
+            grad_pre[span(c), cols] = (total * slope[span(c), cols].astype(F32)).astype(BF16)
+
+    def back_up(c):
+        low = dot_nt(grad_pre[span(c)], b_u[...]).astype(BF16)
+        back_u[span(c)] = low
+
+        @pl.loop(0, F)
+        def _(g):
+            cols = cols_of(g, block)
+            put_part(c, cols, dot_nt(grad_pre[span(c)], up_all[g]) + dot_nn(low, a_u[:, cols]))
+
+    def back_mix(c):
+        low = dot_nt(chunk(grad_branch, c), b_o[...]).astype(BF16)
+        back_o[span(c)] = low
+        total = dot_nn(low, a_o[...])
+        for g in range(F):
+            rows = grad_branch[c, :, :, pl.ds(g * block, block)].reshape(M, block)
+            total += dot_nt(rows, proj_all[g])
+        grad_mixed[span(c)] = total.astype(BF16)
+
+    def back_project(c):
+        lows = []
+        for j in range(3):
+            low = dot_nt(grad_qkv[j, span(c)], b_q(j)[...]).astype(BF16)
+            back_q[j, span(c)] = low
+            lows.append(low)
+
+        @pl.loop(0, F)
+        def _(g):
+            cols = cols_of(g, block)
+            total = dot_nn(lows[0], a_q(0)[:, cols])
+            for j in range(3):
+                if j:
+                    total += dot_nn(lows[j], a_q(j)[:, cols])
+                total += dot_nt(grad_qkv[j, span(c)], qkv_all[j, g])
+            put_part(c, cols, total)
+
+    def own(c):
+        return pl.ds(c * R, R)
+
+    def meet_one(c):
+        total = rs_sum(c) + hidden[c, z].astype(F32) + v_proj[...]
+        unit, rstd = norm_parts(total)
+        unit_one[own(c)] = unit
+        rstd_one[own(c)] = jnp.broadcast_to(rstd, (R, 128))
+        normed[c, z] = (unit * gain_a[...] + shift_a[...]).astype(BF16)
+
+    def meet_two(c):
+        total = rs_sum(c) + unit_one[own(c)] * gain_a[...] + shift_a[...] + v_down[...]
+        unit, rstd = norm_parts(total)
+        layer_out[own(c)] = unit * gain_b[...] + shift_b[...]
+        grad = norm_pull(cotangent[own(c)].astype(F32) * gain_b[...], unit, rstd)
+        grad_own[own(c)] = grad
+        grad_feed[c, z] = grad.astype(BF16)
+
+    def meet_three(c):
+        grad = (grad_own[own(c)] + rs_sum(c)) * gain_a[...]
+        grad = norm_pull(grad, unit_one[own(c)], rstd_one[own(c)][:, :1])
+        grad_own[own(c)] = grad
+        grad_branch[c, z] = grad.astype(BF16)
+
+    def meet_four(c):
+        grad_input[own(c)] = grad_own[own(c)] + rs_sum(c)
+
+    def factor(low, right):
+        return dot_nn(low.astype(F32).T.astype(BF16), right)
+
+    def factors_feed():
+        units_g[pl.ds(0, 16)] = factor(low_u[...], grad_pre[...])
+        units_g[pl.ds(16, 16)] = factor(back_d[...], act[...])
+        wide_g[pl.ds(64, 16)] = factor(back_u[...], normed[...].reshape(S, D))
+        wide_g[pl.ds(80, 16)] = factor(low_d[...], grad_feed[...].reshape(S, D))
+
+    def factors_mix():
+        heads_g[pl.ds(48, 16)] = factor(back_o[...], mixed[...])
+        wide_g[pl.ds(48, 16)] = factor(low_o[...], grad_branch[...].reshape(S, D))
+
+    def factors_project():
+        for j in range(3):
+            heads_g[pl.ds(16 * j, 16)] = factor(low_q[j], grad_qkv[j])
+            wide_g[pl.ds(16 * j, 16)] = factor(back_q[j], hidden[...].reshape(S, D))
+
+    from_low[:, 0] = jnp.zeros((C, R, D), BF16)
+    from_high[:, T - 1] = jnp.zeros((C, R, D), BF16)
+    qkv_g, proj_g, up_g, down_g = gathers
+    def own_hidden(step):
+        return line_copy(hidden_in, hidden.at[:, z], g_up_send if step > 0 else g_dn_send, g_up_recv if step > 0 else g_dn_recv, C, z, step)
+
+    @pl.when(z < T - 1)
+    def _():
+        own_hidden(1).start()
+
+    @pl.when(z > 0)
+    def _():
+        own_hidden(-1).start()
+
+    qkv_g.stage(0)
+    for copy in own_copies:
+        copy.start()
+    schedule(cfg, dict(locals()))
+
+
+def schedule(cfg, env):
+    T, C, K = cfg["T"], cfg["C"], env["K"]
+    rs, ag, hidden = env["rs"], env["ag"], env["hidden"]
+    qkv_g, proj_g, up_g, down_g = env["gathers"]
+    chunks = range(C)
+    for step in range(1, K + 1):
+        qkv_g.stage(step)
+        if step == 1:
+            proj_g.stage(0)
+            ag(hidden, None, 2)
+    if K == 0:
+        proj_g.stage(0)
+    if K >= 1:
+        proj_g.stage(1)
+    up_g.stage(0)
+    if K < 1:
+        ag(hidden, None, 2)
+    for t in range(3, T + 1):
+        ag(hidden, None, t)
+    for step in range(2, K + 1):
+        proj_g.stage(step)
+    down_g.stage(0)
+    qkv_g.finish()
+    for copy in env["own_copies"]:
+        copy.wait()
+    env["project"]()
+    env["attend"]()
+    for step in range(1, K + 1):
+        up_g.stage(step)
+    proj_g.finish()
+    buffers = [env["normed"], env["grad_feed"], env["grad_branch"]]
+    meets = [env["meet_one"], env["meet_two"], env["meet_three"], env["meet_four"]]
+
+    def work(k, c):
+        if k > 0:
+            env["rs_drain"](c)
+        if k == 0:
+            env["mix_out"](c)
+        if k == 1:
+            if c == 0:
+                for step in range(1, K + 1):
+                    down_g.stage(step)
+                up_g.finish()
+            env["feed_up"](c)
+            if c == 0:
+                down_g.finish()
+            env["feed_down"](c)
+        if k == 2:
+            env["back_down"](c)
+            env["back_up"](c)
+        if k == 3:
+            env["back_project"](c)
+        rs(c, 1)
+
+    for k in range(3):
+        for c in chunks:
+            work(k, c)
+        for t in range(2, T):
+            for c in chunks:
+                rs(c, t)
+        for c in chunks:
+            meets[k](c)
+            if k > 0:
+                env["ag_drain"](buffers[k - 1], c)
+            ag(buffers[k], c, 1)
+        for t in range(2, T + 1):
+            for c in chunks:
+                ag(buffers[k], c, t)
+    for c in chunks:
+        env["back_mix"](c)
+    env["attend_back"]()
+    for c in chunks:
+        work(3, c)
+    env["factors_feed"]()
+    env["factors_mix"]()
+    env["factors_project"]()
+    for t in range(2, T):
+        for c in chunks:
+            rs(c, t)
+    for c in chunks:
+        meets[3](c)
+    for c in chunks:
+        env["rs_drain"](c)
+        env["ag_drain"](buffers[2], c)
+    env["ag_drain"](hidden, None)
+    for gather in env["gathers"]:
+        gather.drain()
+
+
+def spread(mesh, body):
     placed = (
         P(("fsdp", "tp"), None),
         P(("fsdp", "tp"), None),
@@ -330,7 +919,7 @@
         P(),
     )
     return jax.shard_map(
-        per_device,
+        body,
         mesh=mesh,
         in_specs=placed,
         out_specs=(
@@ -347,3 +936,111 @@
         ),
         check_vma=False,
     )
+
+
+def chunks_for(rows):
+    return 2 if rows % 32 == 0 else 1
+
+
+def kernel_per_device(F, T):
+    def per_device(
+        hidden_in, cotangent, segment_ids, adapter_set, qkv_weight, qkv_bias, proj_weight, proj_bias,
+        up_weight, up_bias, down_weight, down_bias, norm_gain, norm_bias, qkv_adapt_in, qkv_adapt_out,
+        attn_adapt_in, attn_adapt_out, up_adapt_in, up_adapt_out, down_adapt_in, down_adapt_out,
+    ):
+        Q, D = hidden_in.shape
+        H, FL = qkv_weight.shape[2], up_weight.shape[1]
+        S, C, sets = Q * T, chunks_for(Q), qkv_adapt_in.shape[1]
+        R, block = Q // C, D // F
+        cfg = dict(F=F, T=T, S=S, D=D, H=H, FL=FL, C=C)
+        chosen = adapter_set[0]
+        turn = lambda table: jnp.swapaxes(table, -1, -2)
+        pick = lambda table, axis: choose_set(table, chosen, axis)
+        wide_f = jnp.concatenate(
+            [
+                pick(turn(qkv_adapt_in), 1).reshape(-1, D),
+                pick(attn_adapt_out, 0),
+                pick(turn(up_adapt_in), 0),
+                pick(down_adapt_out, 0),
+            ]
+        )
+        heads_f = jnp.concatenate(
+            [pick(qkv_adapt_out, 1).reshape(-1, H), pick(turn(attn_adapt_in), 0)]
+        )
+        units_f = jnp.concatenate([pick(up_adapt_out, 0), pick(turn(down_adapt_in), 0)])
+        vectors = jnp.stack(
+            [proj_bias, down_bias, norm_gain[0], norm_bias[0], norm_gain[1], norm_bias[1]]
+        ).astype(F32)
+        bias_rows = jnp.stack([qkv_bias[0], jnp.zeros_like(qkv_bias[0]), qkv_bias[1]]).astype(F32)
+        segments = segment_ids[0].reshape(T, C, R).transpose(1, 0, 2).reshape(S)
+        vmem, anywhere = pl.BlockSpec(memory_space=pltpu.VMEM), pl.BlockSpec(memory_space=pl.ANY)
+        dma = pltpu.SemaphoreType.DMA
+        bank = lambda *shape: pltpu.VMEM(shape, BF16)
+        wide_bank = lambda *shape: pltpu.VMEM(shape, F32)
+        scratch = (
+            [bank(C, T, R, D), bank(3, F, block, H), bank(F, H, block), bank(F, block, FL), bank(F, FL, block)]
+            + [bank(3, S, H), bank(H // HEAD, S, S), bank(S, H), bank(C, T, R, D), bank(S, FL), bank(S, FL)]
+            + [bank(C, T, R, D), bank(S, FL), bank(C, T, R, D), bank(S, H), bank(3, S, H)]
+            + [bank(C, T, R, D), bank(C, T, R, D), bank(C, T, R, D)]
+            + [wide_bank(Q, D), wide_bank(Q, 128), wide_bank(Q, D)]
+            + [bank(3, S, RANK), bank(S, RANK), bank(S, RANK), bank(S, RANK)] * 2
+            + [dma((4, 2, F)), dma((4, 2, F))]
+            + [dma((C, T))] * 4
+            + [dma((C + 1, T))] * 4
+            + [dma((5,))]
+        )
+        flops = 2 * S * (4 * D * H + 2 * D * FL) * 2
+        outs = pl.pallas_call(
+            functools.partial(layer_kernel, cfg),
+            out_shape=[
+                jax.ShapeDtypeStruct((Q, D), F32),
+                jax.ShapeDtypeStruct((Q, D), F32),
+                jax.ShapeDtypeStruct((6 * RANK, D), F32),
+                jax.ShapeDtypeStruct((4 * RANK, H), F32),
+                jax.ShapeDtypeStruct((2 * RANK, FL), F32),
+            ],
+            in_specs=[anywhere] + [vmem] * 3 + [anywhere] * 4 + [vmem] * 6,
+            out_specs=[vmem] * 5,
+            scratch_shapes=scratch,
+            compiler_params=pltpu.CompilerParams(
+                collective_id=0, has_side_effects=True, vmem_limit_bytes=62 * 1024 * 1024
+            ),
+            cost_estimate=pl.CostEstimate(flops=flops, bytes_accessed=30000000, transcendentals=0),
+        )(
+            hidden_in.reshape(C, R, D), cotangent, segments[None, :], segments[:, None],
+            qkv_weight, proj_weight, up_weight, down_weight,
+            vectors, up_bias.astype(F32)[None, :], bias_rows, wide_f, heads_f, units_f,
+        )
+        layer_out, grad_input, wide_g, heads_g, units_g = outs
+        onehot = (jnp.arange(sets) == chosen).astype(F32)[:, None, None]
+        wide_t = lax.psum((wide_g * onehot).astype(BF16), ("fsdp", "tp")).astype(F32)
+        heads_t, units_t = lax.psum(
+            ((heads_g * onehot).astype(BF16), (units_g * onehot).astype(BF16)), "fsdp"
+        )
+        heads_t, units_t = heads_t.astype(F32), units_t.astype(F32)
+        trio = lambda table: table.reshape(sets, 3, RANK, -1).transpose(1, 0, 2, 3)
+        return (
+            layer_out,
+            grad_input,
+            turn(trio(wide_t[:, :48])),
+            trio(heads_t[:, :48]),
+            turn(heads_t[:, 48:]),
+            wide_t[:, 48:64],
+            turn(wide_t[:, 64:80]),
+            units_t[:, :16],
+            turn(units_t[:, 16:]),
+            wide_t[:, 80:],
+        )
+
+    return per_device
+
+
+def solution(mesh):
+    F, T = mesh.shape["fsdp"], mesh.shape["tp"]
+
+    def whole(*args):
+        width = args[0].shape[1]
+        fits = F & (F - 1) == 0 and (width // F) % 128 == 0 and T > 1 and F > 1
+        return spread(mesh, kernel_per_device(F, T) if fits else per_device)(*args)
+
+    return whole

time: 993 us -> 624 us (0.63)
  waiting for transfers between devices: 803 us -> 195 us
  Pallas kernels: 0 us -> 376 us
  matrix products: 114 us -> 0 us
  other arithmetic: 32.9 us -> 16.8 us
    pallas_call x0 -> x1, Pallas kernels: none -> 376 us  [per_device(): pl.pallas_call(functools.partial(layer_kernel, cfg), out_shape=[jax.Shape...]
    all_gather x8 -> x0, waiting for transfers between devices: 331 us -> none  [the longest x1 52.8 us: per_device(): lax.all_gather(up_weight, 'fsdp', axis=0, tiled=True)]
    reduce_scatter x4 -> x0, waiting for transfers between devices: 266 us -> none  [the longest x1 76.2 us: per_device(): lax.psum_scatter(mixed_dot(row_part, down_full) + precise_dot(low_part, s...]
    dot_general x38 -> x0, matrix products: 114 us -> none  [the longest x12 36.1 us: precise_dot(): return jnp.dot(left, right, precision=lax.Precision.HIGHEST)]
    unnamed x85 -> x15, local copies, waits for them, and re-layouts: 14.4 us -> 2.48 us
    reduce_sum x8 -> x0, other arithmetic: 10.8 us -> none  [the longest x2 3.42 us: layer_norm(): centred = field_in - centre]
  transfers between devices with their start and end apart: 14 -> 2, of which waited for: 14 -> 2; matrix products, arithmetic and copies ran while one was open for 7% -> 1% of each run, Pallas kernels for 0% -> 0%
where the time goes in v1:
time: 624 us; the launch traced here: 623 us
  Pallas kernels  376 us (60%)
  waiting for transfers between devices  195 us (31%)
  local copies, waits for them, and re-layouts  21.2 us (3%)
  other arithmetic  16.8 us (3%)
  between operations  14.8 us (2%)
    pallas_call x1, Pallas kernels, per_device(): pl.pallas_call(functools.partial(layer_kernel, cfg), out_shape=[jax.Shape...  376 us
    psum x1, waiting for transfers between devices, per_device(): lax.psum((wide_g * onehot).astype(BF16), ('fsdp', 'tp')).astype(F32)  137 us
    psum x1, waiting for transfers between devices, per_device(): lax.psum(((heads_g * onehot).astype(BF16), (units_g * onehot).astype(BF16...  57.2 us
  transfers between devices with their start and end apart: 2, of which 2 were waited for; matrix products, arithmetic and copies ran while one was open for 1% of the time, Pallas kernels for 0%

profile of v1, /device:TPU:0, one launch (start us, length us, event | category | flops | bytes accessed | tf_op | source)
XLA Modules:
  0.0 623.2 jit_solution(9898089110642257319)
XLA Ops:
  7.8 1.3 reduce.3
  9.2 0.9 broadcast_in_dim_reshape.8.refs_3_
  11.5 0.9 dynamic-slice_bitcast_fusion.4
  12.3 0.8 constant_dynamic-slice_fusion
  13.1 0.7 dynamic-slice_bitcast_fusion.5
  13.8 0.7 stack.12
  14.5 0.7 stack.13
  15.2 0.8 fusion.1
  16.7 0.8 fusion.3
  17.5 1.3 broadcast_in_dim.11
  18.8 0.9 dynamic-slice_bitcast_fusion
  19.7 0.9 dynamic-slice_bitcast_fusion.1
  21.9 0.7 maximum_convert_fusion.refs_10_
  22.6 0.8 pad_maximum_fusion.refs_11_
  23.4 375.6 %shard_map.285 = (f32[128,2048]{1,0:T(8,128)}, f32[128,2048]{1,0:T(8,128)}, f32[96,2048]{1,0:T(8,128)}, f32[64,512]{1,0:T(8,128)}, f32[32,2048]{1,0:T(8,128)}) custom-call(bf16[2,64,2048]{2,1,0:T(8,128)(2,1)} %bitcast.56, bf16[128,2048]{1,0:T(8,128)(2,1)} %refs_1_.1, s32[1,512]{1,0:T(1,128)} %broadcast_in_dim_reshape.6.refs_2_, ...), custom_call_target="tpu_custom_call" | custom-call | flops 25769803776 | bytes 30000000 | tf_op jit(solution)/shard_map/pallas_call | solution.py:993
  399.0 2.2 multiply_convert_fusion.1
  401.2 1.8 multiply_convert_fusion.2
  403.1 2.5 multiply_convert_fusion
  405.6 57.2 %all-reduce.6.cloned.1.call-done = (bf16[8,64,512]{2,1,0:T(8,128)(2,1)}, bf16[8,32,2048]{2,1,0:T(8,128)(2,1)}) async-done(((bf16[8,64,512]{2,1,0:T(8,128)(2,1)}, bf16[8,32,2048]{2,1,0:T(8,128)(2,1)}), (bf16[8,64,512]{2,1,0:T(8,128)(2,1)}, bf16[8,32,2048]{2,1,0:T(8,128)(2,1)})) %all-reduce.6.cloned.1.call-update) | async-done | bytes 1572880 | tf_op jit(solution)/shard_map/psum | solution.py:1017
  462.8 1.2 slice.57
  464.0 1.2 convert_element_type.38
  465.4 1.1 slice.61
  466.5 0.9 copy.43
  467.4 0.7 slice_bitcast_fusion.2
  468.2 1.0 slice_bitcast_fusion
  469.2 137.5 %all-reduce.4.cloned.1.call-done = bf16[8,96,2048]{2,1,0:T(8,128)(2,1)} async-done(((bf16[8,96,2048]{2,1,0:T(8,128)(2,1)}), bf16[8,96,2048]{2,1,0:T(8,128)(2,1)}) %all-reduce.4.cloned.1.call-update) | async-done | bytes 3145744 | tf_op jit(solution)/shard_map/psum | solution.py:1016
  606.7 2.9 convert_element_type.36
  609.5 1.1 slice_bitcast_fusion.1
  611.0 1.9 copy.42
  612.9 1.6 fusion
  614.4 1.0 copy.51
  615.4 1.0 copy.52
  (29 shorter events, 4.1 us)
Async XLA Ops:
  7.2 4.2 copy-start
  7.2 455.6 %all-reduce.6.cloned.1.call-start = ((), (), s32[]{:S(2)}) async-start(), calls=%async_computation.1 | async-start | bytes 3145728 | tf_op jit(solution)/shard_map/psum | solution.py:1017
  399.0 4.1 copy-start.5
  403.1 203.6 %all-reduce.4.cloned.1.call-start = ((), (), s32[]{:S(2)}) async-start(), calls=%async_computation | async-start | bytes 6291456 | tf_op jit(solution)/shard_map/psum | solution.py:1016
  462.8 2.4 copy-start.2
  606.7 4.0 copy-start.1
  612.9 1.6 copy-start.4
  612.9 2.5 copy-start.3
Sparse Core Ops, SparseCore 0:
  403.2 59.5 all-reduce.5
  469.8 136.8 all-reduce.3

commit v2 on v1

--- a/solution.py
+++ b/solution.py
@@ -414,13 +414,17 @@
     M = T * R
     NT = min(256, FL)
     (
-        hidden_in, cotangent, seg_row, seg_col, qkv_w, proj_w, up_w, down_w,
-        vectors, up_bias, qkv_bias, wide_f, heads_f, units_f,
-        layer_out, grad_input, wide_g, heads_g, units_g,
+        hidden_in, cotangent, seg_row, seg_col, chosen, qkv_w, proj_w, up_w, down_w,
+        side_bias, up_bias, qkv_bias, gains, shifts,
+        q_in, q_out, o_in, o_out, u_in, u_out, d_in, d_out,
+        layer_out, grad_input, feed_all, units_all, mix_all, heads_all,
         hidden, qkv_all, proj_all, up_all, down_all,
         qkv, probs, mixed, normed, act, slope, grad_feed, grad_pre, grad_branch, grad_mixed, grad_qkv,
         part, from_low, from_high, unit_one, rstd_one, grad_own,
         low_q, low_o, low_u, low_d, back_q, back_o, back_u, back_d,
+        wide_f, heads_f, units_f, wide_stage, heads_stage, units_stage,
+        feed_part, feed_land, feed_full, mix_part, mix_land, mix_full, units_g, heads_g,
+        stage_sem, deal_send, deal_recv, share_send, share_recv,
         w_send, w_recv, up_send, up_recv, dn_send, dn_recv, g_up_send, g_up_recv, g_dn_send, g_dn_recv,
         own_sem,
     ) = refs
@@ -431,23 +435,10 @@
     for bit in bits:
         pl.semaphore_signal(barrier, inc=1, device_id=(flip(f, bit), z), device_id_type=MESH)
 
-    @pl.when(z > 0)
-    def _():
-        pl.semaphore_signal(barrier, inc=1, device_id=(f, z - 1), device_id_type=MESH)
-
-    @pl.when(z < T - 1)
-    def _():
-        pl.semaphore_signal(barrier, inc=1, device_id=(f, z + 1), device_id_type=MESH)
-
-    inside = (z > 0) & (z < T - 1)
-
-    @pl.when(inside)
-    def _():
-        pl.semaphore_wait(barrier, len(bits) + 2)
-
-    @pl.when(jnp.logical_not(inside))
-    def _():
-        pl.semaphore_wait(barrier, len(bits) + 1)
+    turns = [lax.rem(z + k, T) for k in range(T)]
+    for k in range(1, T):
+        pl.semaphore_signal(barrier, inc=1, device_id=(f, turns[k]), device_id_type=MESH)
+    pl.semaphore_wait(barrier, len(bits) + T - 1)
 
     rows_of = lambda total, half: pl.ds(half * (total // 2), total // 2)
     gathers = [
@@ -456,6 +447,13 @@
         Gather(2, lambda h: up_w.at[rows_of(block, h)], lambda g, h: up_all.at[g, rows_of(block, h)], w_send, w_recv, f, z, F),
         Gather(3, lambda h: down_w.at[rows_of(FL, h)], lambda g, h: down_all.at[g, rows_of(FL, h)], w_send, w_recv, f, z, F),
     ]
+    pair = lambda ref, n: lambda h: ref.at[..., rows_of(n, h), :]
+    pair_all = lambda ref, n: lambda g, h: ref.at[g, ..., rows_of(n, h), :]
+    for k, (shard, whole) in enumerate(
+        [(feed_full, feed_all), (units_g, units_all), (mix_full, mix_all), (heads_g, heads_all)]
+    ):
+        n = shard.shape[-2]
+        gathers.append(Gather(4 + k, pair(shard, n), pair_all(whole, n), w_send, w_recv, f, z, F))
     K = gathers[0].steps
     own_copies = [
         pltpu.make_async_copy(hidden_in, hidden.at[:, z], own_sem.at[0]),
@@ -464,6 +462,56 @@
         pltpu.make_async_copy(up_w, up_all.at[f], own_sem.at[3]),
         pltpu.make_async_copy(down_w, down_all.at[f], own_sem.at[4]),
     ]
+    own_grads = [
+        pltpu.make_async_copy(feed_full, feed_all.at[f], own_sem.at[5]),
+        pltpu.make_async_copy(units_g, units_all.at[f], own_sem.at[6]),
+        pltpu.make_async_copy(mix_full, mix_all.at[f], own_sem.at[7]),
+        pltpu.make_async_copy(heads_g, heads_all.at[f], own_sem.at[8]),
+    ]
+
+    def deal_copy(which, part_ref, land_ref, k):
+        return pltpu.make_async_remote_copy(
+            src_ref=part_ref.at[turns[k]], dst_ref=land_ref.at[k - 1],
+            send_sem=deal_send.at[which, k - 1], recv_sem=deal_recv.at[which, k - 1],
+            device_id=(f, turns[k]), device_id_type=MESH,
+        )
+
+    def share_copy(which, full_ref, k, place):
+        return pltpu.make_async_remote_copy(
+            src_ref=full_ref.at[place], dst_ref=full_ref.at[place],
+            send_sem=share_send.at[which, k - 1], recv_sem=share_recv.at[which, k - 1],
+            device_id=(f, turns[k]), device_id_type=MESH,
+        )
+
+    exchanges = [(feed_part, feed_land, feed_full), (mix_part, mix_land, mix_full)]
+
+    def deal(which):
+        for k in range(1, T):
+            deal_copy(which, exchanges[which][0], exchanges[which][1], k).start()
+
+    def share(which):
+        part_ref, land_ref, full_ref = exchanges[which]
+        total = part_ref[z].astype(F32)
+        for k in range(1, T):
+            deal_copy(which, part_ref, land_ref, k).wait_recv()
+            total += land_ref[k - 1].astype(F32)
+        full_ref[z] = total.astype(BF16)
+        for k in range(1, T):
+            share_copy(which, full_ref, k, z).start()
+
+    def pass_on(which):
+        for k in range(1, T):
+            share_copy(which, exchanges[which][2], k, turns[T - k]).wait_recv()
+        for k in (2 * which, 2 * which + 1):
+            own_grads[k].start()
+            gathers[4 + k].stage(0)
+
+    def pass_drain(which):
+        for k in range(1, T):
+            deal_copy(which, exchanges[which][0], exchanges[which][1], k).wait_send()
+            share_copy(which, exchanges[which][2], k, z).wait_send()
+        for k in (2 * which, 2 * which + 1):
+            own_grads[k].wait()
 
     def line_copy(src, dst, send, recv, c, q, step):
         return pltpu.make_async_remote_copy(
@@ -583,12 +631,43 @@
             def _(q=q):
                 ag_copy(buffer, c, q, -1).wait_send()
 
-    a_q = lambda j: wide_f.at[pl.ds(16 * j, 16)]
-    b_o, a_u, b_d = (wide_f.at[pl.ds(16 * k, 16)] for k in (3, 4, 5))
-    b_q = lambda j: heads_f.at[pl.ds(16 * j, 16)]
-    a_o = heads_f.at[pl.ds(48, 16)]
-    b_u, a_d = (units_f.at[pl.ds(16 * k, 16)] for k in (0, 1))
-    v_proj, v_down, gain_a, shift_a, gain_b, shift_b = (vectors.at[pl.ds(k, 1)] for k in range(6))
+    a_q = lambda j: wide_f.at[j]
+    b_o, a_u, b_d = wide_f.at[3], wide_f.at[4], wide_f.at[5]
+    b_q = lambda j: heads_f.at[j]
+    a_o = heads_f.at[3]
+    b_u, a_d = units_f.at[0], units_f.at[1]
+    line = lambda ref, k: ref[pl.ds(k, 1)].astype(F32)
+    sets = q_in.shape[1]
+    pick = (lax.broadcasted_iota(jnp.int32, (sets, 128), 0) == chosen[...]).astype(F32)
+
+    def stage_copies(s):
+        slot = s % 2
+        pairs = [
+            (q_in.at[:, s], wide_stage.at[slot, pl.ds(0, 3)]),
+            (o_out.at[s], wide_stage.at[slot, 3]),
+            (u_in.at[s], wide_stage.at[slot, 4]),
+            (d_out.at[s], wide_stage.at[slot, 5]),
+            (q_out.at[:, s], heads_stage.at[slot, pl.ds(0, 3)]),
+            (o_in.at[s], heads_stage.at[slot, 3]),
+            (u_out.at[s], units_stage.at[slot, 0]),
+            (d_in.at[s], units_stage.at[slot, 1]),
+        ]
+        return [
+            pltpu.make_async_copy(src, dst, stage_sem.at[slot, k])
+            for k, (src, dst) in enumerate(pairs)
+        ]
+
+    def choose(s):
+        for copy in stage_copies(s):
+            copy.wait()
+        weight = pick[s : s + 1, :1].astype(BF16)
+        for stage, held in ((wide_stage, wide_f), (heads_stage, heads_f), (units_stage, units_f)):
+            for k in range(held.shape[0]):
+                term = stage[s % 2, k] * weight
+                held[k] = term if s == 0 else held[k] + term
+        if s + 2 < sets:
+            for copy in stage_copies(s + 2):
+                copy.start()
 
     def chunk(buffer, c):
         return buffer[c].reshape(M, buffer.shape[-1])
@@ -606,7 +685,9 @@
             def _(n, j=j, low_j=low_j):
                 cols = cols_of(n, width)
                 rows = dot_nn(hidden[...].reshape(S, D), qkv_all[j, :, :, cols].reshape(D, width))
-                rows += dot_nn(low_j, b_q(j)[:, cols]) + qkv_bias[pl.ds(j, 1), cols]
+                rows += dot_nn(low_j, b_q(j)[:, cols])
+                if j != 1:
+                    rows += qkv_bias[pl.ds(j // 2, 1), cols].astype(F32)
                 qkv[j, :, cols] = rows.astype(BF16)
 
     scale = 1.0 / math.sqrt(HEAD)
@@ -674,7 +755,7 @@
         def _(n):
             cols = cols_of(n, NT)
             pre = dot_nn(chunk(normed, c), up_all[:, :, cols].reshape(D, NT))
-            pre += dot_nn(low, b_u[:, cols]) + up_bias[:, cols]
+            pre += dot_nn(low, b_u[:, cols]) + up_bias[:, cols].astype(F32)
             square = pre * pre
             bend = jnp.tanh(ROOT * (pre + 0.044715 * square * pre))
             half = 0.5 * (1.0 + bend)
@@ -743,22 +824,22 @@
         return pl.ds(c * R, R)
 
     def meet_one(c):
-        total = rs_sum(c) + hidden[c, z].astype(F32) + v_proj[...]
+        total = rs_sum(c) + hidden[c, z].astype(F32) + line(side_bias, 0)
         unit, rstd = norm_parts(total)
         unit_one[own(c)] = unit
         rstd_one[own(c)] = jnp.broadcast_to(rstd, (R, 128))
-        normed[c, z] = (unit * gain_a[...] + shift_a[...]).astype(BF16)
+        normed[c, z] = (unit * line(gains, 0) + line(shifts, 0)).astype(BF16)
 
     def meet_two(c):
-        total = rs_sum(c) + unit_one[own(c)] * gain_a[...] + shift_a[...] + v_down[...]
+        total = rs_sum(c) + unit_one[own(c)] * line(gains, 0) + line(shifts, 0) + line(side_bias, 1)
         unit, rstd = norm_parts(total)
-        layer_out[own(c)] = unit * gain_b[...] + shift_b[...]
-        grad = norm_pull(cotangent[own(c)].astype(F32) * gain_b[...], unit, rstd)
+        layer_out[own(c)] = unit * line(gains, 1) + line(shifts, 1)
+        grad = norm_pull(cotangent[own(c)].astype(F32) * line(gains, 1), unit, rstd)
         grad_own[own(c)] = grad
         grad_feed[c, z] = grad.astype(BF16)
 
     def meet_three(c):
-        grad = (grad_own[own(c)] + rs_sum(c)) * gain_a[...]
+        grad = (grad_own[own(c)] + rs_sum(c)) * line(gains, 0)
         grad = norm_pull(grad, unit_one[own(c)], rstd_one[own(c)][:, :1])
         grad_own[own(c)] = grad
         grad_branch[c, z] = grad.astype(BF16)
@@ -767,26 +848,35 @@
         grad_input[own(c)] = grad_own[own(c)] + rs_sum(c)
 
     def factor(low, right):
-        return dot_nn(low.astype(F32).T.astype(BF16), right)
+        return dot_nn(low.astype(F32).T.astype(BF16), right).astype(BF16)
+
+    def by_columns(low, right, place, row):
+        turned = low.astype(F32).T.astype(BF16)
+        for q in range(T):
+            cols = pl.ds(q * H, H)
+            rows = right[:, :, :, cols].reshape(S, H)
+            place[q, pl.ds(row, 16)] = dot_nn(turned, rows).astype(BF16)
 
     def factors_feed():
         units_g[pl.ds(0, 16)] = factor(low_u[...], grad_pre[...])
         units_g[pl.ds(16, 16)] = factor(back_d[...], act[...])
-        wide_g[pl.ds(64, 16)] = factor(back_u[...], normed[...].reshape(S, D))
-        wide_g[pl.ds(80, 16)] = factor(low_d[...], grad_feed[...].reshape(S, D))
+        by_columns(back_u[...], normed, feed_part, 0)
+        by_columns(low_d[...], grad_feed, feed_part, 16)
 
     def factors_mix():
         heads_g[pl.ds(48, 16)] = factor(back_o[...], mixed[...])
-        wide_g[pl.ds(48, 16)] = factor(low_o[...], grad_branch[...].reshape(S, D))
+        by_columns(low_o[...], grad_branch, mix_part, 48)
 
     def factors_project():
         for j in range(3):
             heads_g[pl.ds(16 * j, 16)] = factor(low_q[j], grad_qkv[j])
-            wide_g[pl.ds(16 * j, 16)] = factor(back_q[j], hidden[...].reshape(S, D))
+            by_columns(back_q[j], hidden, mix_part, 16 * j)
+        marks = jnp.concatenate([pick[:, :1], jnp.zeros((32 - sets, 1), F32)])
+        heads_g[pl.ds(64, 32)] = jnp.broadcast_to(marks, (32, H)).astype(BF16)
 
     from_low[:, 0] = jnp.zeros((C, R, D), BF16)
     from_high[:, T - 1] = jnp.zeros((C, R, D), BF16)
-    qkv_g, proj_g, up_g, down_g = gathers
+    qkv_g = gathers[0]
     def own_hidden(step):
         return line_copy(hidden_in, hidden.at[:, z], g_up_send if step > 0 else g_dn_send, g_up_recv if step > 0 else g_dn_recv, C, z, step)
 
@@ -799,7 +889,7 @@
         own_hidden(-1).start()
 
     qkv_g.stage(0)
-    for copy in own_copies:
+    for copy in own_copies + stage_copies(0) + stage_copies(1):
         copy.start()
     schedule(cfg, dict(locals()))
 
@@ -807,13 +897,17 @@
 def schedule(cfg, env):
     T, C, K = cfg["T"], cfg["C"], env["K"]
     rs, ag, hidden = env["rs"], env["ag"], env["hidden"]
-    qkv_g, proj_g, up_g, down_g = env["gathers"]
+    qkv_g, proj_g, up_g, down_g = env["gathers"][:4]
     chunks = range(C)
+    for s in range(2):
+        env["choose"](s)
     for step in range(1, K + 1):
         qkv_g.stage(step)
         if step == 1:
             proj_g.stage(0)
             ag(hidden, None, 2)
+            for s in range(2, 5):
+                env["choose"](s)
     if K == 0:
         proj_g.stage(0)
     if K >= 1:
@@ -821,6 +915,10 @@
     up_g.stage(0)
     if K < 1:
         ag(hidden, None, 2)
+        for s in range(2, 5):
+            env["choose"](s)
+    for s in range(5, env["sets"]):
+        env["choose"](s)
     for t in range(3, T + 1):
         ag(hidden, None, t)
     for step in range(2, K + 1):
@@ -831,8 +929,8 @@
         copy.wait()
     env["project"]()
     env["attend"]()
-    for step in range(1, K + 1):
-        up_g.stage(step)
+    if K:
+        up_g.stage(1)
     proj_g.finish()
     buffers = [env["normed"], env["grad_feed"], env["grad_branch"]]
     meets = [env["meet_one"], env["meet_two"], env["meet_three"], env["meet_four"]]
@@ -844,11 +942,13 @@
             env["mix_out"](c)
         if k == 1:
             if c == 0:
-                for step in range(1, K + 1):
-                    down_g.stage(step)
+                for step in range(2, K + 1):
+                    up_g.stage(step)
                 up_g.finish()
             env["feed_up"](c)
             if c == 0:
+                for step in range(2, K + 1):
+                    down_g.stage(step)
                 down_g.finish()
             env["feed_down"](c)
         if k == 2:
@@ -858,37 +958,64 @@
             env["back_project"](c)
         rs(c, 1)
 
+    def meet(k, c):
+        meets[k](c)
+        if k > 0:
+            env["ag_drain"](buffers[k - 1], c)
+        ag(buffers[k], c, 1)
+
+    steps = []
     for k in range(3):
+        steps.append((work, k))
+        steps += [(lambda t, c: rs(c, t), t) for t in range(2, T)]
+        steps.append((meet, k))
+        steps += [(lambda kt, c: ag(buffers[kt[0]], c, kt[1]), (k, t)) for t in range(2, T + 1)]
+    steps.append((lambda unused, c: env["back_mix"](c), None))
+    lag = cfg["lag"]
+    for at in range(len(steps) + lag * (C - 1)):
+        if at == 1 and K:
+            down_g.stage(1)
         for c in chunks:
-            work(k, c)
-        for t in range(2, T):
-            for c in chunks:
-                rs(c, t)
-        for c in chunks:
-            meets[k](c)
-            if k > 0:
-                env["ag_drain"](buffers[k - 1], c)
-            ag(buffers[k], c, 1)
-        for t in range(2, T + 1):
-            for c in chunks:
-                ag(buffers[k], c, t)
-    for c in chunks:
-        env["back_mix"](c)
+            if 0 <= at - lag * c < len(steps):
+                step, detail = steps[at - lag * c]
+                step(detail, c)
+        if at == 2 * (2 * T - 1) + 1 + lag * (C - 1):
+            env["factors_feed"]()
+            env["deal"](0)
+    env["share"](0)
     env["attend_back"]()
+    env["pass_on"](0)
     for c in chunks:
         work(3, c)
-    env["factors_feed"]()
     env["factors_mix"]()
     env["factors_project"]()
+    env["deal"](1)
+    grads = env["gathers"][4:]
     for t in range(2, T):
         for c in chunks:
             rs(c, t)
+        if t == 2:
+            env["share"](1)
+            for gather in grads[:2]:
+                if K:
+                    gather.stage(1)
+    env["pass_on"](1)
     for c in chunks:
         meets[3](c)
+    for step in range(2, K + 1):
+        for gather in grads[:2]:
+            gather.stage(step)
+    for step in range(1, K + 1):
+        for gather in grads[2:]:
+            gather.stage(step)
+    for gather in grads:
+        gather.finish()
     for c in chunks:
         env["rs_drain"](c)
         env["ag_drain"](buffers[2], c)
     env["ag_drain"](hidden, None)
+    for which in range(2):
+        env["pass_drain"](which)
     for gather in env["gathers"]:
         gather.drain()
 
@@ -939,7 +1066,31 @@
 
 
 def chunks_for(rows):
-    return 2 if rows % 32 == 0 else 1
+    return max(c for c in (1, 2, 4) if rows % (16 * c) == 0)
+
+
+def place_kernel(feed_all, units_all, mix_all, heads_all, *outs):
+    q_in, q_out, o_in, o_out, u_in, u_out, d_in, d_out = outs
+    F, T, _, H = feed_all.shape
+    sets = o_in.shape[0]
+    for ref in outs:
+        ref[...] = jnp.zeros_like(ref)
+    order = lax.broadcasted_iota(jnp.int32, (32, 1), 0).astype(F32)
+    for g in range(F):
+        marks = heads_all[g, pl.ds(64, 32), pl.ds(0, 128)][:, :1].astype(F32)
+        s = jnp.minimum(jnp.sum(marks * order).astype(jnp.int32), sets - 1)
+        for t in range(T):
+            cols = pl.ds(t * H, H)
+            u_in[s, :, cols] += feed_all[g, t, pl.ds(0, 16)].astype(F32)
+            d_out[s, :, cols] += feed_all[g, t, pl.ds(16, 16)].astype(F32)
+            o_out[s, :, cols] += mix_all[g, t, pl.ds(48, 16)].astype(F32)
+            for j in range(3):
+                q_in[j, s, :, cols] += mix_all[g, t, pl.ds(16 * j, 16)].astype(F32)
+        for j in range(3):
+            q_out[j, s] += heads_all[g, pl.ds(16 * j, 16)].astype(F32)
+        o_in[s] += heads_all[g, pl.ds(48, 16)].astype(F32)
+        u_out[s] += units_all[g, pl.ds(0, 16)].astype(F32)
+        d_in[s] += units_all[g, pl.ds(16, 16)].astype(F32)
 
 
 def kernel_per_device(F, T):
@@ -952,26 +1103,8 @@
         H, FL = qkv_weight.shape[2], up_weight.shape[1]
         S, C, sets = Q * T, chunks_for(Q), qkv_adapt_in.shape[1]
         R, block = Q // C, D // F
-        cfg = dict(F=F, T=T, S=S, D=D, H=H, FL=FL, C=C)
-        chosen = adapter_set[0]
+        cfg = dict(F=F, T=T, S=S, D=D, H=H, FL=FL, C=C, lag=1)
         turn = lambda table: jnp.swapaxes(table, -1, -2)
-        pick = lambda table, axis: choose_set(table, chosen, axis)
-        wide_f = jnp.concatenate(
-            [
-                pick(turn(qkv_adapt_in), 1).reshape(-1, D),
-                pick(attn_adapt_out, 0),
-                pick(turn(up_adapt_in), 0),
-                pick(down_adapt_out, 0),
-            ]
-        )
-        heads_f = jnp.concatenate(
-            [pick(qkv_adapt_out, 1).reshape(-1, H), pick(turn(attn_adapt_in), 0)]
-        )
-        units_f = jnp.concatenate([pick(up_adapt_out, 0), pick(turn(down_adapt_in), 0)])
-        vectors = jnp.stack(
-            [proj_bias, down_bias, norm_gain[0], norm_bias[0], norm_gain[1], norm_bias[1]]
-        ).astype(F32)
-        bias_rows = jnp.stack([qkv_bias[0], jnp.zeros_like(qkv_bias[0]), qkv_bias[1]]).astype(F32)
         segments = segment_ids[0].reshape(T, C, R).transpose(1, 0, 2).reshape(S)
         vmem, anywhere = pl.BlockSpec(memory_space=pltpu.VMEM), pl.BlockSpec(memory_space=pl.ANY)
         dma = pltpu.SemaphoreType.DMA
@@ -984,10 +1117,16 @@
             + [bank(C, T, R, D), bank(C, T, R, D), bank(C, T, R, D)]
             + [wide_bank(Q, D), wide_bank(Q, 128), wide_bank(Q, D)]
             + [bank(3, S, RANK), bank(S, RANK), bank(S, RANK), bank(S, RANK)] * 2
-            + [dma((4, 2, F)), dma((4, 2, F))]
+            + [bank(6, RANK, D), bank(4, RANK, H), bank(2, RANK, FL)]
+            + [bank(2, 6, RANK, D), bank(2, 4, RANK, H), bank(2, 2, RANK, FL)]
+            + [bank(T, 32, H), bank(T - 1, 32, H), bank(T, 32, H)]
+            + [bank(T, 64, H), bank(T - 1, 64, H), bank(T, 64, H)]
+            + [bank(32, FL), bank(96, H)]
+            + [dma((2, 8))] + [dma((2, T - 1))] * 4
+            + [dma((8, 2, F)), dma((8, 2, F))]
             + [dma((C, T))] * 4
             + [dma((C + 1, T))] * 4
-            + [dma((5,))]
+            + [dma((9,))]
         )
         flops = 2 * S * (4 * D * H + 2 * D * FL) * 2
         outs = pl.pallas_call(
@@ -995,12 +1134,13 @@
             out_shape=[
                 jax.ShapeDtypeStruct((Q, D), F32),
                 jax.ShapeDtypeStruct((Q, D), F32),
-                jax.ShapeDtypeStruct((6 * RANK, D), F32),
-                jax.ShapeDtypeStruct((4 * RANK, H), F32),
-                jax.ShapeDtypeStruct((2 * RANK, FL), F32),
+                jax.ShapeDtypeStruct((F, T, 32, H), BF16),
+                jax.ShapeDtypeStruct((F, 32, FL), BF16),
+                jax.ShapeDtypeStruct((F, T, 64, H), BF16),
+                jax.ShapeDtypeStruct((F, 96, H), BF16),
             ],
-            in_specs=[anywhere] + [vmem] * 3 + [anywhere] * 4 + [vmem] * 6,
-            out_specs=[vmem] * 5,
+            in_specs=[anywhere] + [vmem] * 4 + [anywhere] * 4 + [vmem] * 5 + [anywhere] * 8,
+            out_specs=[vmem] * 2 + [anywhere] * 4,
             scratch_shapes=scratch,
             compiler_params=pltpu.CompilerParams(
                 collective_id=0, has_side_effects=True, vmem_limit_bytes=62 * 1024 * 1024
@@ -1008,28 +1148,25 @@
             cost_estimate=pl.CostEstimate(flops=flops, bytes_accessed=30000000, transcendentals=0),
         )(
             hidden_in.reshape(C, R, D), cotangent, segments[None, :], segments[:, None],
-            qkv_weight, proj_weight, up_weight, down_weight,
-            vectors, up_bias.astype(F32)[None, :], bias_rows, wide_f, heads_f, units_f,
-        )
-        layer_out, grad_input, wide_g, heads_g, units_g = outs
-        onehot = (jnp.arange(sets) == chosen).astype(F32)[:, None, None]
-        wide_t = lax.psum((wide_g * onehot).astype(BF16), ("fsdp", "tp")).astype(F32)
-        heads_t, units_t = lax.psum(
-            ((heads_g * onehot).astype(BF16), (units_g * onehot).astype(BF16)), "fsdp"
-        )
-        heads_t, units_t = heads_t.astype(F32), units_t.astype(F32)
-        trio = lambda table: table.reshape(sets, 3, RANK, -1).transpose(1, 0, 2, 3)
+            adapter_set[None, :], qkv_weight, proj_weight, up_weight, down_weight,
+            jnp.stack([proj_bias, down_bias]), up_bias[None, :], qkv_bias, norm_gain, norm_bias,
+            turn(qkv_adapt_in), qkv_adapt_out, turn(attn_adapt_in), attn_adapt_out,
+            turn(up_adapt_in), up_adapt_out, turn(down_adapt_in), down_adapt_out,
+        )
+        layer_out, grad_input = outs[:2]
+        table = lambda *shape: jax.ShapeDtypeStruct(shape, F32)
+        q_in, q_out, o_in, o_out, u_in, u_out, d_in, d_out = pl.pallas_call(
+            place_kernel,
+            out_shape=[
+                table(3, sets, RANK, D), table(3, sets, RANK, H), table(sets, RANK, H), table(sets, RANK, D),
+                table(sets, RANK, D), table(sets, RANK, FL), table(sets, RANK, FL), table(sets, RANK, D),
+            ],
+            in_specs=[vmem] * 4,
+            out_specs=[vmem] * 8,
+            compiler_params=pltpu.CompilerParams(vmem_limit_bytes=40 * 1024 * 1024),
+        )(*outs[2:])
         return (
-            layer_out,
-            grad_input,
-            turn(trio(wide_t[:, :48])),
-            trio(heads_t[:, :48]),
-            turn(heads_t[:, 48:]),
-            wide_t[:, 48:64],
-            turn(wide_t[:, 64:80]),
-            units_t[:, :16],
-            turn(units_t[:, 16:]),
-            wide_t[:, 80:],
+            layer_out, grad_input, turn(q_in), q_out, turn(o_in), o_out, turn(u_in), u_out, turn(d_in), d_out,
         )
 
     return per_device
@@ -1040,7 +1177,7 @@
 
     def whole(*args):
         width = args[0].shape[1]
-        fits = F & (F - 1) == 0 and (width // F) % 128 == 0 and T > 1 and F > 1
+        fits = F & (F - 1) == 0 and (width // F) % 128 == 0 and T > 1 and F > 1 and args[14].shape[1] <= 32
         return spread(mesh, kernel_per_device(F, T) if fits else per_device)(*args)
 
     return whole

time: 624 us -> 335 us (0.54)
  waiting for transfers between devices: 195 us -> 0 us
  Pallas kernels: 376 us -> 317 us
  other arithmetic: 16.8 us -> 1.97 us
  between operations: 14.8 us -> 1.32 us
  local copies, waits for them, and re-layouts: 21.2 us -> 12.7 us
    psum x2 -> x0, waiting for transfers between devices: 195 us -> none  [the longest x1 137 us: per_device(): lax.psum((wide_g * onehot).astype(BF16), ('fsdp', 'tp')).astype(F32)]
    pallas_call x1, Pallas kernels: 376 us -> 312 us  [per_device(): pl.pallas_call(functools.partial(layer_kernel, cfg), out_shape=[jax.Shape...]
    convert_element_type x9 -> x0, other arithmetic: 12.1 us -> none  [the longest x1 2.87 us: per_device(): lax.psum((wide_g * onehot).astype(BF16), ('fsdp', 'tp')).astype(F32)]
  transfers between devices with their start and end apart: 2 -> 0, of which waited for: 2 -> 0; matrix products, arithmetic and copies ran while one was open for 1% -> 0% of each run, Pallas kernels for 0% -> 0%
where the time goes in v2:
time: 335 us; the launch traced here: 333 us
  Pallas kernels  317 us (95%)
  local copies, waits for them, and re-layouts  12.7 us (4%)
    pallas_call x1, Pallas kernels, per_device(): pl.pallas_call(functools.partial(layer_kernel, cfg), out_shape=[jax.Shape...  312 us
    unnamed x15, local copies, waits for them, and re-layouts  8.25 us

profile of v2, /device:TPU:0, one launch (start us, length us, event | category | flops | bytes accessed | tf_op | source)
XLA Modules:
  0.0 333.4 jit_solution(13617628463691571416)
XLA Ops:
  1.3 0.5 broadcast.3
  1.8 1.3 reduce.3
  3.1 0.1 reshape_squeeze.3
  3.2 0.7 broadcast_in_dim_reshape.6.refs_2_
  3.9 0.7 stack.9
  4.6 1.3 broadcast_in_dim.7.refs_10_
  5.9 0.7 stack.10
  6.6 0.6 pad_maximum_fusion.refs_9_
  7.2 1.0 broadcast_in_dim_reshape.8.refs_3_
  8.2 312.1 %shard_map.285 = (f32[128,2048]{1,0:T(8,128)}, f32[128,2048]{1,0:T(8,128)}, bf16[8,4,32,512]{3,2,1,0:T(8,128)(2,1)}, bf16[8,32,2048]{2,1,0:T(8,128)(2,1)}, bf16[...) custom-call(bf16[4,32,2048]{2,1,0:T(8,128)(2,1)} %bitcast.20, bf16[128,2048]{1,0:T(8,128)(2,1)} %refs_1_.1, ...), custom_call_target="tpu_custom_call" | custom-call | flops 25769803776 | bytes 30000000 | tf_op jit(solution)/shard_map/pallas_call | solution.py:1132
  320.3 0.0 copy-start
  320.3 1.6 copy-done
  321.9 0.0 copy-start.1
  321.9 1.2 copy-done.1
  323.1 0.0 copy-start.2
  323.1 1.2 copy-done.2
  324.4 0.0 copy-start.3
  324.4 1.1 copy-done.3
  325.5 0.0 copy-start.5
  325.5 5.3 %shard_map.286 = (f32[3,8,16,2048]{3,2,1,0:T(8,128)}, f32[3,8,16,512]{3,2,1,0:T(8,128)}, f32[8,16,512]{2,1,0:T(8,128)}, f32[8,16,2048]{2,1,0:T(8,128)}, f32[8,16...) custom-call(bf16[8,4,32,512]{3,2,1,0:T(8,128)(2,1)S(1)} %copy-done.1, ...), custom_call_target="tpu_custom_call" | custom-call | tf_op jit(solution)/shard_map/pallas_call | solution.py:1158
  330.8 0.0 copy-start.4
  330.8 0.0 copy-done.5
  330.8 1.0 copy.40
  331.8 0.6 copy-done.4
  332.4 1.0 copy.41
  (1 shorter events, 0.0 us)
Async XLA Ops:
  320.3 1.6 copy-start
  321.9 1.2 copy-start.1
  323.1 1.2 copy-start.2
  324.4 1.1 copy-start.3
  325.5 5.3 %copy-start.5 = (f32[128,2048]{1,0:T(8,128)S(1)}, f32[128,2048]{1,0:T(8,128)}, u32[]{:S(2)}) copy-start(f32[128,2048]{1,0:T(8,128)} %get-tuple-element.48) | copy-start | bytes 3145732
  330.8 1.6 copy-start.4
